TPU v7x, 32 devices: a whole 2x2x4 slice. The times are simulated.
32 devices in a mesh: ctx: 4 (over x, core), tp: 8 (over z, y).
Axes of the slice: x: 2, y: 2, z: 4, core: 2. Of those that a mesh axis runs over, the one named last changes fastest.
Arguments:
- residual: bfloat16 [1024, 8192], P('ctx', 'tp'), may hold values from -8 to 8
- queries: bfloat16 [1024, 8192], P('ctx', 'tp'), may hold values from -15 to 15
- keys_values: bfloat16 [1024, 2048], P('ctx'), may hold values from -6 to 6
- out_weight: bfloat16 [8192, 8192], P('tp', 'ctx'), may hold values from -0.09375 to 0.09375
- norm_gain: float32 [8192], replicated, may hold values from 0.1 to 1.9
- cache_weight: bfloat16 [8192, 2048], P(None, 'tp'), may hold values from -0.0625 to 0.0625
- positions: int32 [1024], P('ctx'), may hold values from 0 to 2047, as said below
- keep_rows: int32 [1024], P('ctx'), may hold values from 0 to 255, as said below
- kept_count: int32 [4], P('ctx'), may hold values from 64 to 256, as said below
Outputs:
- kept_hidden: bfloat16 [1024, 8192], P('ctx', 'tp')
- kept_cache: bfloat16 [1024, 2048], P('ctx', 'tp')
Inputs may be any that keep to these rules, and one draw needn't show every extreme that they name: `keep_rows`: within every shard of ctx the 256 entries are a permutation of the shard's local rows: first its kept rows in ascending order, as many as its kept_count, then its dropped rows in ascending order. `kept_count`: for every even shard index e, shards e and e + 1 keep 2 * 160 rows together. `positions`: strictly increasing along the tokens.
All inputs are finite; a program needn't handle non-finite values.
Results may differ from a plain program's by a relative error of at most 0.019.
Values may be sent and summed in bfloat16 or wider, within the bound.
A program may use at most 64 MiB of HBM per device.

v0:
```python
import math

import jax
import jax.numpy as jnp
from jax import lax
from jax.sharding import PartitionSpec as P

D = 8192
HQ = 64
KVH = 8
HD = 128


THETA = 1000000.0
EPS = 1e-06


def rotate_pairs(cache_rows, position_ids, first_col, head_dim):
    pair_count = cache_rows.shape[1] // 2
    columns = first_col + 2 * jnp.arange(pair_count, dtype=jnp.int32)
    within = columns % (2 * head_dim)
    is_key = within < head_dim
    exponent = jnp.where(is_key, within, 0).astype(jnp.float32) / head_dim
    frequency = jnp.power(jnp.float32(THETA), -exponent)
    angles = position_ids.astype(jnp.float32)[:, None] * frequency[None, :]
    paired = cache_rows.reshape(cache_rows.shape[0], pair_count, 2)
    first_half = paired[..., 0]
    second = paired[..., 1]
    cosine = jnp.cos(angles)
    sine_rows = jnp.sin(angles)
    turned_first = first_half * cosine - second * sine_rows
    turned_second = second * cosine + first_half * sine_rows
    turned = jnp.stack(
        [jnp.where(is_key, turned_first, first_half), jnp.where(is_key, turned_second, second)], -1
    )
    return turned.reshape(cache_rows.shape)


def shards(
    residual,
    queries,
    keys_values,
    out_weight,
    norm_gain,
    cache_weight,
    positions,
    keep_rows,
    kept_count,
):
    row_count = residual.shape[0]
    ctx_index = lax.axis_index("ctx")
    tp_index = lax.axis_index("tp")
    head_count = queries.shape[1] // HD
    kv_head = tp_index * head_count // (HQ // KVH)
    head_block = lax.dynamic_slice_in_dim(keys_values, kv_head * 2 * HD, 2 * HD, 1)
    key_rows = head_block[:, :HD]
    value_rows = head_block[:, HD:]
    query_rows = queries.reshape(row_count, head_count, HD)
    own_index = ctx_index * row_count + jnp.arange(row_count, dtype=jnp.int32)
    score_scale = 1.0 / math.sqrt(HD)
    running_max = jnp.full((row_count, head_count), -1e30, jnp.float32)
    key_block = lax.all_gather(key_rows, "ctx", axis=0, tiled=True)
    value_block = lax.all_gather(value_rows, "ctx", axis=0, tiled=True)
    block_rows = key_block.shape[0]
    scores = (
        jnp.einsum("rgd,kd->rgk", query_rows, key_block, preferred_element_type=jnp.float32)
        * score_scale
    )
    visible = jnp.arange(block_rows, dtype=jnp.int32)[None, :] <= own_index[:, None]
    visible = visible[:, None, :]
    scores = jnp.where(visible, scores, -1e30)
    new_max = jnp.maximum(running_max, jnp.max(scores, axis=-1))
    weights = jnp.where(visible, jnp.exp(scores - new_max[..., None]), 0.0)
    new_sum = jnp.sum(weights, axis=-1)
    update = jnp.einsum(
        "rgk,kd->rgd", weights.astype(jnp.bfloat16), value_block, preferred_element_type=jnp.float32
    )
    attended = (
        (update / new_sum[..., None]).reshape(row_count, head_count * HD).astype(jnp.bfloat16)
    )
    own_count = kept_count[0]
    valid_rows = jnp.arange(row_count, dtype=jnp.int32) < own_count
    partials = jnp.dot(
        attended,
        lax.all_gather(out_weight, "ctx", axis=1, tiled=True),
        preferred_element_type=jnp.float32,
    )
    group_sums = lax.psum_scatter(
        partials.astype(jnp.bfloat16), "tp", scatter_dimension=1, tiled=True
    ).astype(jnp.float32)
    hidden = (residual.astype(jnp.float32) + group_sums).astype(jnp.bfloat16)
    feat_width = hidden.shape[1]
    wide_hidden = hidden.astype(jnp.float32)
    square_total = lax.psum(jnp.sum(wide_hidden * wide_hidden, axis=-1), "tp")
    inverse = lax.rsqrt(square_total / D + EPS)
    gain_part = lax.dynamic_slice_in_dim(norm_gain, tp_index * feat_width, feat_width)
    normed = (wide_hidden * inverse[:, None] * gain_part[None, :]).astype(jnp.bfloat16)
    gathered = lax.all_gather(normed, "tp", axis=1, tiled=True)
    cache_rows = jnp.dot(gathered, cache_weight, preferred_element_type=jnp.float32)
    cache_rot = rotate_pairs(cache_rows, positions, tp_index * cache_rows.shape[1], HD).astype(
        jnp.bfloat16
    )
    kept_flags = jnp.zeros((row_count,), jnp.int32).at[keep_rows].set(valid_rows.astype(jnp.int32))
    kept_mask = kept_flags[:, None] > 0
    kept_hidden = jnp.where(kept_mask, hidden, jnp.zeros_like(hidden))
    kept_cache = jnp.where(kept_mask, cache_rot, jnp.zeros_like(cache_rot))
    return (kept_hidden, kept_cache)


def solution(mesh):
    in_specs = (
        P("ctx", "tp"),
        P("ctx", "tp"),
        P("ctx", None),
        P("tp", "ctx"),
        P(),
        P(None, "tp"),
        P("ctx"),
        P("ctx"),
        P("ctx"),
    )
    out_specs = (P("ctx", "tp"), P("ctx", "tp"))
    return jax.shard_map(shards, mesh=mesh, in_specs=in_specs, out_specs=out_specs, check_vma=False)
```

profile of v0, /device:TPU:0, one launch (start us, length us, event | category | flops | bytes accessed | tf_op | source)
XLA Modules:
  0.0 331.1 jit_solution(13383946528182603673)
XLA Ops:
  7.2 0.0 copy-start
  7.2 0.0 all-gather.3.cloned.1.call-start
  7.2 0.7 all-gather.3.cloned.1.call-update
  7.9 0.0 reduce-scatter.2.cloned.1.call-start
  8.0 0.9 constant_dynamic-slice_fusion.1
  8.9 7.2 %all_gather.12 = bf16[1024,128]{1,0:T(8,128)(2,1)S(1)} all-gather(bf16[256,128]{1,0:T(8,128)(2,1)S(1)} %get-tuple-element.5), channel_id=1, replica_groups=mesh['ctx'=4,'tp'=8] {'ctx'}, dimensions={0}, use_global_device_ids=true | all-gather | bytes 327680 | tf_op jit(solution)/shard_map/all_gather | solution.py:62
  16.1 5.8 %all_gather.13 = bf16[1024,128]{1,0:T(8,128)(2,1)S(1)} all-gather(bf16[256,128]{1,0:T(8,128)(2,1)S(1)} %get-tuple-element.4), channel_id=1, replica_groups=mesh['ctx'=4,'tp'=8] {'ctx'}, dimensions={0}, use_global_device_ids=true | all-gather | bytes 327680 | tf_op jit(solution)/shard_map/all_gather | solution.py:63
  21.9 0.2 iota_compare_fusion
  22.1 0.0 copy-done
  22.1 1.4 fusion
  23.6 2.0 fusion.1
  25.6 2.1 divide_convert_fusion
  27.7 90.5 %all-gather.3.cloned.1.call-done = bf16[1024,8192]{1,0:T(8,128)(2,1)} async-done(((bf16[1024,2048]{1,0:T(8,128)(2,1)}), bf16[1024,8192]{1,0:T(8,128)(2,1)}) %all-gather.3.cloned.1.call-update) | async-done | bytes 16777232 | tf_op jit(solution)/shard_map/all_gather | solution.py:85
  118.2 0.0 copy-start.1
  118.2 0.0 copy-start.2
  118.2 0.0 copy-start.3
  118.2 12.1 %convolution_convert_fusion = bf16[256,8192]{1,0:T(8,128)(2,1)} fusion(bf16[256,1024]{0,1:T(8,128)(2,1)S(1)} %bitcast.41, bf16[1024,8192]{1,0:T(8,128)(2,1)} %all-gather.3.cloned.1.call-done), kind=kOutput, calls=%fused_computation.1 | convolution fusion | flops 4297064448 | bytes 21495808 | tf_op jit(solution)/shard_map/dot_general | solution.py:83
  130.3 0.0 reduce-scatter.2.cloned.1.call-update
  130.3 0.0 all-gather.5.cloned.1.call-start
  130.4 0.7 dynamic_slice.7
  131.1 87.7 %reduce-scatter.2.cloned.1.call-done = bf16[256,1024]{1,0:T(8,128)(2,1)} async-done(((bf16[256,8192]{1,0:T(8,128)(2,1)}), bf16[256,1024]{1,0:T(8,128)(2,1)}) %reduce-scatter.2.cloned.1.call-update) | async-done | bytes 524304 | tf_op jit(solution)/shard_map/reduce_scatter | solution.py:88
  218.8 0.0 copy-done.1
  218.8 1.3 fusion.6
  220.1 20.2 %psum.7 = f32[256]{0:T(256)S(1)} all-reduce(f32[256]{0:T(256)S(1)} %fusion.6), channel_id=1, replica_groups=mesh['ctx'=4,'tp'=8] {'tp'}, use_global_device_ids=true, to_apply=%region_5.6 | all-reduce | flops 256 | bytes 2048 | tf_op jit(solution)/shard_map/psum | solution.py:94
  240.3 2.1 fusion.8
  242.4 0.0 all-gather.5.cloned.1.call-update
  242.4 0.0 copy-done.2
  243.1 0.0 copy-done.3
  243.1 1.6 scatter_custom_fusion
  244.7 2.0 broadcast_select_fusion
  246.7 66.4 %all-gather.5.cloned.1.call-done = bf16[256,8192]{1,0:T(8,128)(2,1)} async-done(((bf16[256,1024]{1,0:T(8,128)(2,1)}), bf16[256,8192]{1,0:T(8,128)(2,1)}) %all-gather.5.cloned.1.call-update) | async-done | bytes 4194320 | tf_op jit(solution)/shard_map/all_gather | solution.py:98
  313.2 5.2 %fusion.24 = f32[256,256]{0,1:T(8,128)S(1)} fusion(bf16[256,8192]{1,0:T(8,128)(2,1)} %all-gather.5.cloned.1.call-done, bf16[8192,256]{1,0:T(8,128)(2,1)} %param.14), kind=kOutput, calls=%fused_computation.50 | convolution fusion | flops 1073741824 | bytes 8650752 | tf_op jit(solution)/shard_map/dot_general | solution.py:99
  318.4 0.1 reshape.163
  318.5 4.9 %fusion.16 = (bf16[256,128,1]{0,2,1:T(2,128)(2,1)S(1)}, bf16[256,128,1]{0,2,1:T(2,128)(2,1)S(1)}) fusion(pred[128]{0:T(512)(128)(4,1)S(1)} %broadcast_compare_fusion.1, f32[256,128,2]{0,2,1:T(2,128)S(1)} %reshape.163, f32[256]{0:T(256)S(1)} %convert_element_type.54, f32[128]{0:T(128)S(1)} %negate_power_fusion), kind=kLoop, calls=%fused_computation.29 | loop fusion | flops 360448 | bytes 394880 | tf_op jit(solution)/shard_map/convert
  323.4 0.3 pad_maximum_fusion
  323.7 0.1 convert_element_type.56
  323.8 0.8 copy.18
  (10 shorter events, 0.1 us)
Async XLA Ops:
  7.2 14.9 %copy-start = (bf16[256,1024]{1,0:T(8,128)(2,1)S(1)}, bf16[256,1024]{1,0:T(8,128)(2,1)}, u32[]{:S(2)}) copy-start(bf16[256,1024]{1,0:T(8,128)(2,1)} %param.10) | copy-start | bytes 1572868
  7.2 111.0 %all-gather.3.cloned.1.call-start = ((), (), s32[]{:S(2)}) async-start(), calls=%async_computation.1 | async-start | bytes 20971520 | tf_op jit(solution)/shard_map/all_gather | solution.py:85
  7.9 210.9 %reduce-scatter.2.cloned.1.call-start = ((), (), s32[]{:S(2)}) async-start(), calls=%async_computation.2 | async-start | bytes 4718592 | tf_op jit(solution)/shard_map/reduce_scatter | solution.py:88
  118.2 100.6 %copy-start.1 = (bf16[256,1024]{1,0:T(8,128)(2,1)S(1)}, bf16[256,1024]{1,0:T(8,128)(2,1)}, u32[]{:S(2)}) copy-start(bf16[256,1024]{1,0:T(8,128)(2,1)} %param.9) | copy-start | bytes 1572868
  118.2 124.2 %copy-start.2 = (s32[256]{0:T(256)S(1)}, s32[256]{0:T(256)}, u32[]{:S(2)}) copy-start(s32[256]{0:T(256)} %param.15) | copy-start | bytes 3076
  118.2 124.8 %copy-start.3 = (s32[256]{0:T(256)S(1)}, s32[256]{0:T(256)}, u32[]{:S(2)}) copy-start(s32[256]{0:T(256)} %param.16) | copy-start | bytes 3076
  130.3 182.8 %all-gather.5.cloned.1.call-start = ((), (), s32[]{:S(2)}) async-start(), calls=%async_computation.3 | async-start | bytes 4718592 | tf_op jit(solution)/shard_map/all_gather | solution.py:98
Sparse Core Ops, SparseCore 0:
  9.6 108.6 all-gather.2
  130.5 88.3 reduce-scatter.1
  242.5 70.6 all-gather.4
where the time goes:
time: 331 us
  waiting for transfers between devices  245 us (74%)
  blocking collectives  33.2 us (10%)
  matrix products  20.8 us (6%)
  between operations  14.6 us (4%)
  other arithmetic  12.8 us (4%)
  local copies, waits for them, and re-layouts  4.14 us (1%)
    all_gather x1, waiting for transfers between devices, shards(): lax.all_gather(out_weight, 'ctx', axis=1, tiled=True)  90.5 us
    reduce_scatter x1, waiting for transfers between devices, shards(): lax.psum_scatter(partials.astype(jnp.bfloat16), 'tp', scatter_dimension=1...  87.7 us
    all_gather x1, waiting for transfers between devices, shards(): gathered = lax.all_gather(normed, 'tp', axis=1, tiled=True)  66.4 us
    psum x1, blocking collectives, shards(): square_total = lax.psum(jnp.sum(wide_hidden * wide_hidden, axis=-1), 'tp')  20.2 us
    dot_general x1, matrix products, shards(): jnp.dot(attended, lax.all_gather(out_weight, 'ctx', axis=1, tiled=True),...  12.1 us
    all_gather x1, blocking collectives, shards(): key_block = lax.all_gather(key_rows, 'ctx', axis=0, tiled=True)  7.19 us
  transfers between devices with their start and end apart: 3, of which 3 were waited for; matrix products, arithmetic and copies ran while one was open for 3% of the time, Pallas kernels for 0%

commit v1 on v0

--- a/solution.py
+++ b/solution.py
@@ -3,6 +3,8 @@
 import jax
 import jax.numpy as jnp
 from jax import lax
+from jax.experimental import pallas as pl
+from jax.experimental.pallas import tpu as pltpu
 from jax.sharding import PartitionSpec as P
 
 D = 8192
@@ -107,6 +109,372 @@
     return (kept_hidden, kept_cache)
 
 
+KEPT = 160
+Z = 4
+MESH = pl.DeviceIdType.MESH
+BF = jnp.bfloat16
+F32 = jnp.float32
+
+
+def fused_kernel(
+    q_ref, r_ref, kv_hbm, w_hbm, cw_hbm, gain_ref, slot_row, slot_col,
+    hid_out, cache_out,
+    kvbuf, w_ref, cw_ref, qown, qrecv, rown, rrecv, resbuf, attb, ownp, ysend, yrecv,
+    zsum, zrecv, hbuf, cmsg, crecv, cbuf, hpair,
+    loc_sem, kv_s, kv_r, q_s, q_r, res_s, res_r, att_s, att_r, y_s, y_r, z_s, z_r,
+    ag_s, ag_r, ay_s, ay_r, c_s, c_r, row_s, row_r, fin_s, fin_r,
+):
+    c = lax.axis_index("ctx")
+    t = lax.axis_index("tp")
+    p, k = c // 2, c % 2
+    z, y = t // 2, t % 2
+    rows = q_ref.shape[0]
+
+    def ctx_peer(i):
+        return ((p + i // 2) % 2) * 2 + (k + i % 2) % 2
+
+    def z_peer(d):
+        return (z + d) % Z
+
+    sib = ctx_peer(1)
+    ydev = (c, 2 * z + 1 - y)
+    is_root = c == z
+    pending = []
+
+    def remote(src, dst, ss, rs, dev):
+        return pltpu.make_async_remote_copy(
+            src_ref=src, dst_ref=dst, send_sem=ss, recv_sem=rs, device_id=dev, device_id_type=MESH
+        )
+
+    def send(src, dst, ss, rs, dev):
+        copy = remote(src, dst, ss, rs, dev)
+        copy.start()
+        pending.append(copy)
+        return copy
+
+    w_copy = pltpu.make_async_copy(w_hbm, w_ref, loc_sem.at[0])
+    w_copy.start()
+    feat = cw_ref.shape[0]
+    cw_copy = pltpu.make_async_copy(
+        cw_hbm.at[pl.ds(pl.multiple_of(c * feat, feat), feat)], cw_ref, loc_sem.at[1]
+    )
+    cw_copy.start()
+    own_kv = kvbuf.at[pl.ds(pl.multiple_of(c * rows, rows), rows)]
+    kv_copy = pltpu.make_async_copy(
+        kv_hbm.at[:, pl.ds(pl.multiple_of(t * 2 * HD, 2 * HD), 2 * HD)], own_kv, loc_sem.at[2]
+    )
+    kv_copy.start()
+
+    barrier = pltpu.get_barrier_semaphore()
+    partners = [(ctx_peer(i), t) for i in (1, 2, 3)]
+    partners += [(c, z_peer(d) * 2 + y) for d in (1, 2, 3)] + [ydev]
+    for dev in partners:
+        pl.semaphore_signal(barrier, inc=1, device_id=dev, device_id_type=MESH)
+    pl.semaphore_wait(barrier, len(partners))
+
+    slots = slot_row[...]
+    slot_at = lax.broadcasted_iota(jnp.int32, (KEPT, rows), 0)
+    pick_sib = jnp.where(slots == slot_at + (1 - k) * KEPT, 1.0, 0.0).astype(BF)
+    pick_own = jnp.where(slots == slot_at + k * KEPT, 1.0, 0.0).astype(BF)
+    row_id = lax.broadcasted_iota(jnp.int32, (rows, HD), 0).astype(F32)
+    lane = lax.broadcasted_iota(jnp.int32, (rows, HD), 1)
+    tags = jnp.where(lane == 0, row_id, jnp.where(lane == 1, 1.0, 0.0)).astype(BF)
+    width = q_ref.shape[1]
+
+    def pick(sel, what):
+        return jnp.dot(sel, what, preferred_element_type=F32).astype(BF)
+
+    kv_copy.wait()
+    kv_copies = [
+        send(own_kv, own_kv, kv_s.at[i - 1], kv_r.at[i - 1], (ctx_peer(i), t)) for i in (2, 3, 1)
+    ]
+    qown[0, :, :width] = pick(pick_sib, q_ref[...])
+    qown[0, :, width:] = pick(pick_sib, tags)
+    q_copy = send(qown.at[0], qrecv, q_s.at[0], q_r.at[0], (sib, t))
+    rown[0] = pick(pick_sib, r_ref[...])
+    r_copy = send(rown.at[0], rrecv, q_s.at[1], q_r.at[1], (sib, t))
+    qown[1, :, :width] = pick(pick_own, q_ref[...])
+    qown[1, :, width:] = pick(pick_own, tags)
+    rown[1] = pick(pick_own, r_ref[...])
+
+    q_copy.wait_recv()
+    own_tag = qown[1, :, width:].astype(F32)
+    sib_tag = qrecv[:, width:].astype(F32)
+    first_own = (c * rows).astype(F32)
+    first_sib = (sib * rows).astype(F32)
+    limit = (
+        own_tag[:, 0:1] + first_own * own_tag[:, 1:2] + sib_tag[:, 0:1] + first_sib * sib_tag[:, 1:2]
+    )
+    qown[1, :, :width] = qown[1, :, :width] + qrecv[:, :width]
+
+    r_copy.wait_recv()
+    rown[1] = rown[1] + rrecv[...]
+    res_slot = ((p + z // 2) % 2) * 2 + (k + z) % 2
+    res_copy = remote(
+        rown.at[1], resbuf.at[res_slot], res_s, res_r.at[res_slot], (z, t)
+    )
+
+    @pl.when(is_root)
+    def _():
+        resbuf[0] = rown[1]
+
+    @pl.when(jnp.logical_not(is_root))
+    def _():
+        res_copy.start()
+
+    for copy in kv_copies:
+        copy.wait_recv()
+    total = kvbuf.shape[0]
+    col_id = lax.broadcasted_iota(jnp.int32, (KEPT, total), 1).astype(F32)
+    seen = col_id <= limit
+    scale = 1.0 / math.sqrt(HD)
+    keys = kvbuf[:, :HD]
+    values = kvbuf[:, HD:]
+    for h in range(width // HD):
+        cols = slice(h * HD, (h + 1) * HD)
+        s = lax.dot_general(
+            qown[1, :, cols], keys, (((1,), (1,)), ((), ())), preferred_element_type=F32
+        ) * scale
+        s = jnp.where(seen, s, -1e30)
+        top = jnp.max(s, axis=1, keepdims=True)
+        e = jnp.where(seen, jnp.exp(s - top), 0.0)
+        den = jnp.sum(e, axis=1, keepdims=True)
+        mixed = jnp.dot(e.astype(BF), values, preferred_element_type=F32)
+        attb[0, :, cols] = (mixed / den).astype(BF)
+
+    att_cp = send(attb.at[0], attb.at[2], att_s.at[0], att_r.at[0], (ctx_peer(2), t))
+    att_sib = send(attb.at[0], attb.at[1], att_s.at[1], att_r.at[1], (sib, t))
+    half = Z * 256
+    own_cols = pl.ds(pl.multiple_of(y * half, half), half)
+    far_cols = pl.ds(pl.multiple_of((1 - y) * half, half), half)
+    w_copy.wait()
+    fwd = {}
+    ys, zs, ags, ays, cs = {}, {}, {}, {}, {}
+
+    def stage_a(i):
+        if i == 1:
+            att_sib.wait_recv()
+        if i == 2:
+            att_cp.wait_recv()
+            fwd[0] = send(attb.at[2], attb.at[3], att_s.at[2], att_r.at[2], (sib, t))
+        if i == 3:
+            fwd[0].wait_recv()
+        ysend[i] = jnp.dot(attb[i], w_ref[:, far_cols], preferred_element_type=F32).astype(BF)
+        ys[i] = send(ysend.at[i], yrecv.at[i], y_s.at[i], y_r.at[i], ydev)
+        ownp[i] = jnp.dot(attb[i], w_ref[:, own_cols], preferred_element_type=F32)
+
+    def stage_b(i):
+        ys[i].wait_recv()
+
+        @pl.when(is_root)
+        def _():
+            if i > 0:
+                remote(
+                    rown.at[1], resbuf.at[i], res_s, res_r.at[i], (ctx_peer(i), t)
+                ).wait_recv()
+            ownp[i] = ownp[i] + resbuf[i].astype(F32)
+
+        for j in range(Z):
+            cols = slice(j * 256, (j + 1) * 256)
+            zsum[i, j] = (ownp[i, :, cols] + yrecv[i, :, cols].astype(F32)).astype(BF)
+        for d in (2, 1, 3):
+            zs[i, d] = send(
+                zsum.at[i, z_peer(d)], zrecv.at[i, d - 1], z_s.at[i, d - 1], z_r.at[i, d - 1],
+                (c, z_peer(d) * 2 + y),
+            )
+
+    def stage_c(i):
+        for d in (1, 2, 3):
+            zs[i, d].wait_recv()
+        hid = zsum[i, z].astype(F32)
+        for d in range(Z - 1):
+            hid = hid + zrecv[i, d].astype(F32)
+        hbuf[i, y, z] = hid.astype(BF)
+        for d in (2, 1, 3):
+            ags[i, d] = send(
+                hbuf.at[i, y, z], hbuf.at[i, y, z], ag_s.at[i, d - 1], ag_r.at[i, d - 1],
+                (c, z_peer(d) * 2 + y),
+            )
+
+    def row_copy(i):
+        return remote(
+            hbuf.at[i, y], hpair.at[(k + i % 2) % 2], row_s.at[i], row_r, (ctx_peer(i), t)
+        )
+
+    def stage_d(i):
+        for d in (1, 2, 3):
+            ags[i, d].wait_recv()
+        ays[i] = send(hbuf.at[i, y], hbuf.at[i, y], ay_s.at[i], ay_r.at[i], ydev)
+
+        @pl.when(is_root)
+        def _():
+            if i == 0:
+                hpair[k] = hbuf[i, y]
+            else:
+                row_copy(i).start()
+
+    gains = gain_ref[c]
+
+    def stage_e(i):
+        ays[i].wait_recv()
+        acc = jnp.zeros((KEPT, 256), F32)
+        squares = jnp.zeros((KEPT, 1), F32)
+        for q in range(2 * Z):
+            wide = hbuf[i, q // Z, q % Z].astype(F32)
+            squares = squares + jnp.sum(wide * wide, axis=1, keepdims=True)
+            acc = acc + jnp.dot(
+                (wide * gains[q : q + 1, :]).astype(BF),
+                cw_ref[q * 256 : (q + 1) * 256, :],
+                preferred_element_type=F32,
+            )
+        if i == 0:
+            return acc, squares
+        coarse = squares.astype(BF).astype(F32)
+        at = lax.broadcasted_iota(jnp.int32, (KEPT, HD), 1)
+        cmsg[i - 1, :, :256] = acc.astype(BF)
+        cmsg[i - 1, :, 256:] = jnp.where(
+            at == 0, coarse, jnp.where(at == 1, squares - coarse, 0.0)
+        ).astype(BF)
+        cs[i] = send(
+            cmsg.at[i - 1], crecv.at[i - 1], c_s.at[i - 1], c_r.at[i - 1], (ctx_peer(i), t)
+        )
+        return None
+
+    stage_a(0)
+    stage_a(1)
+    stage_b(0)
+    stage_a(2)
+    stage_b(1)
+    stage_c(0)
+    stage_a(3)
+    stage_b(2)
+    stage_c(1)
+    stage_d(0)
+    stage_b(3)
+    stage_c(2)
+    stage_d(1)
+    cw_copy.wait()
+    acc, squares = stage_e(0)
+    stage_c(3)
+    stage_d(2)
+    stage_e(1)
+    stage_d(3)
+    stage_e(2)
+
+    @pl.when(jnp.logical_not(is_root))
+    def _():
+        row_copy(1).wait_recv()
+
+    pair_copy = send(hpair.at[k], hpair.at[k], fin_s.at[0], fin_r.at[0], (sib, t))
+    stage_e(3)
+    slots_c = slot_col[...]
+    place_at = lax.broadcasted_iota(jnp.int32, (rows, KEPT), 1)
+    place = [jnp.where(slots_c == place_at + kk * KEPT, 1.0, 0.0).astype(BF) for kk in range(2)]
+    pair_copy.wait_recv()
+    for j in range(Z):
+        hid_out[:, j * 256 : (j + 1) * 256] = (
+            jnp.dot(place[0], hpair[0, j], preferred_element_type=F32)
+            + jnp.dot(place[1], hpair[1, j], preferred_element_type=F32)
+        ).astype(BF)
+    for i in (1, 2, 3):
+        cs[i].wait_recv()
+        got = crecv[i - 1, :, 256:].astype(F32)
+        acc = acc + crecv[i - 1, :, :256].astype(F32)
+        squares = squares + got[:, 0:1] + got[:, 1:2]
+    cbuf[k] = (acc * lax.rsqrt(squares / D + EPS)).astype(BF)
+    last = send(cbuf.at[k], cbuf.at[k], fin_s.at[1], fin_r.at[1], (sib, t))
+    last.wait_recv()
+    cache_out[...] = (
+        jnp.dot(place[0], cbuf[0], preferred_element_type=F32)
+        + jnp.dot(place[1], cbuf[1], preferred_element_type=F32)
+    ).astype(BF)
+
+    for copy in pending:
+        copy.wait_send()
+
+    @pl.when(jnp.logical_not(is_root))
+    def _():
+        res_copy.wait_send()
+
+    @pl.when(is_root)
+    def _():
+        for i in (1, 2, 3):
+            row_copy(i).wait_send()
+
+
+def rotate_head(raw, position_ids):
+    column = jnp.arange(raw.shape[1], dtype=jnp.int32)
+    within = column - column % 2
+    is_key = column < HD
+    exponent = jnp.where(is_key, within, 0).astype(F32) / HD
+    frequency = jnp.power(jnp.float32(THETA), -exponent)
+    angles = position_ids.astype(F32)[:, None] * frequency[None, :]
+    cosine = jnp.where(is_key, jnp.cos(angles), 1.0)
+    sine = jnp.where(is_key, jnp.sin(angles), 0.0)
+    partner = jnp.where(column % 2 == 0, -jnp.roll(raw, -1, axis=1), jnp.roll(raw, 1, axis=1))
+    return raw * cosine + partner * sine
+
+
+def fused_shards(
+    residual, queries, keys_values, out_weight, norm_gain, cache_weight, positions, keep_rows, kept_count
+):
+    rows, width = queries.shape
+    ctx_index = lax.axis_index("ctx")
+    own_count = kept_count[0]
+    base = jnp.where(ctx_index % 2 == 0, 0, 2 * KEPT - own_count)
+    order = jnp.arange(rows, dtype=jnp.int32)
+    at = jnp.where(order < own_count, base + order + 1, 0)
+    slot = jnp.sum(jnp.where(keep_rows[None, :] == order[:, None], at[None, :], 0), axis=1) - 1
+    feat = out_weight.shape[1]
+    n_ctx = D // feat
+    dma = pltpu.SemaphoreType.DMA
+    vmem = pl.BlockSpec(memory_space=pltpu.VMEM)
+    hbm = pl.BlockSpec(memory_space=pl.ANY)
+    kept_hidden, raw = pl.pallas_call(
+        fused_kernel,
+        out_shape=(
+            jax.ShapeDtypeStruct((rows, width), BF),
+            jax.ShapeDtypeStruct((rows, 2 * HD), BF),
+        ),
+        in_specs=[vmem, vmem, hbm, hbm, hbm, vmem, vmem, vmem],
+        out_specs=(vmem, vmem),
+        scratch_shapes=[
+            pltpu.VMEM((n_ctx * rows, 2 * HD), BF),
+            pltpu.VMEM(out_weight.shape, BF),
+            pltpu.VMEM((feat, 2 * HD), BF),
+            pltpu.VMEM((2, KEPT, width + HD), BF),
+            pltpu.VMEM((KEPT, width + HD), BF),
+            pltpu.VMEM((2, KEPT, width), BF),
+            pltpu.VMEM((KEPT, width), BF),
+            pltpu.VMEM((4, KEPT, width), BF),
+            pltpu.VMEM((4, KEPT, width), BF),
+            pltpu.VMEM((4, KEPT, width), F32),
+            pltpu.VMEM((4, KEPT, width), BF),
+            pltpu.VMEM((4, KEPT, width), BF),
+            pltpu.VMEM((4, Z, KEPT, 256), BF),
+            pltpu.VMEM((4, Z - 1, KEPT, 256), BF),
+            pltpu.VMEM((4, 2, Z, KEPT, 256), BF),
+            pltpu.VMEM((3, KEPT, 256 + HD), BF),
+            pltpu.VMEM((3, KEPT, 256 + HD), BF),
+            pltpu.VMEM((2, KEPT, 256), BF),
+            pltpu.VMEM((2, Z, KEPT, 256), BF),
+            dma((3,)), dma((3,)), dma((3,)), dma((2,)), dma((2,)), dma, dma((4,)),
+            dma((3,)), dma((3,)), dma((4,)), dma((4,)), dma((4, 3)), dma((4, 3)),
+            dma((4, 3)), dma((4, 3)), dma((4,)), dma((4,)), dma((3,)), dma((3,)),
+            dma((4,)), dma, dma((2,)), dma((2,)),
+        ],
+        compiler_params=pltpu.CompilerParams(
+            collective_id=0, has_side_effects=True, vmem_limit_bytes=48 * 1024 * 1024
+        ),
+        cost_estimate=pl.CostEstimate(flops=6_000_000_000, bytes_accessed=8_000_000, transcendentals=1_400_000),
+    )(
+        queries, residual, keys_values, out_weight, cache_weight,
+        norm_gain.reshape(n_ctx, feat // 256, 256), slot[None, :], slot[:, None],
+    )
+    kept_cache = rotate_head(raw.astype(F32), positions).astype(BF)
+    return (kept_hidden, kept_cache)
+
+
 def solution(mesh):
     in_specs = (
         P("ctx", "tp"),
@@ -120,4 +488,6 @@
         P("ctx"),
     )
     out_specs = (P("ctx", "tp"), P("ctx", "tp"))
-    return jax.shard_map(shards, mesh=mesh, in_specs=in_specs, out_specs=out_specs, check_vma=False)
+    fits = mesh.shape["ctx"] == 4 and mesh.shape["tp"] == 8
+    body = fused_shards if fits else shards
+    return jax.shard_map(body, mesh=mesh, in_specs=in_specs, out_specs=out_specs, check_vma=False)

time: 331 us -> 112 us (0.34)
  waiting for transfers between devices: 245 us -> 0 us
  Pallas kernels: 0 us -> 101 us
  blocking collectives: 33.2 us -> 0 us
  matrix products: 20.8 us -> 0 us
  between operations: 14.6 us -> 1.34 us
  other arithmetic: 12.8 us -> 3.37 us
    all_gather x2 -> x0, waiting for transfers between devices: 157 us -> none  [the longest x1 90.5 us: shards(): lax.all_gather(out_weight, 'ctx', axis=1, tiled=True)]
    pallas_call x0 -> x1, Pallas kernels: none -> 101 us  [fused_shards(): pl.pallas_call(fused_kernel, out_shape=(jax.ShapeDtypeStruct((rows, width...]
    reduce_scatter x1 -> x0, waiting for transfers between devices: 87.7 us -> none  [shards(): lax.psum_scatter(partials.astype(jnp.bfloat16), 'tp', scatter_dimension=1...]
    dot_general x4 -> x0, matrix products: 20.8 us -> none  [the longest x1 12.1 us: shards(): jnp.dot(attended, lax.all_gather(out_weight, 'ctx', axis=1, tiled=True),...]
    psum x1 -> x0, blocking collectives: 20.2 us -> none  [shards(): square_total = lax.psum(jnp.sum(wide_hidden * wide_hidden, axis=-1), 'tp')]
    all_gather x2 -> x0, blocking collectives: 13 us -> none  [the longest x1 7.19 us: shards(): key_block = lax.all_gather(key_rows, 'ctx', axis=0, tiled=True)]
    another operation x3 -> x0, other arithmetic: 5.16 us -> none
    unnamed x9 -> x7, local copies, waits for them, and re-layouts: 0.78 us -> 4.1 us
  transfers between devices with their start and end apart: 3 -> 0, of which waited for: 3 -> 0; matrix products, arithmetic and copies ran while one was open for 3% -> 0% of each run, Pallas kernels for 0% -> 0%
where the time goes in v1:
time: 112 us; the launch traced here: 111 us
  Pallas kernels  101 us (90%)
  local copies, waits for them, and re-layouts  5.2 us (5%)
  other arithmetic  3.37 us (3%)
  between operations  1.34 us (1%)
    pallas_call x1, Pallas kernels, fused_shards(): pl.pallas_call(fused_kernel, out_shape=(jax.ShapeDtypeStruct((rows, width...  101 us
    unnamed x7, local copies, waits for them, and re-layouts  4.1 us

profile of v1, /device:TPU:0, one launch (start us, length us, event | category | flops | bytes accessed | tf_op | source)
XLA Modules:
  0.0 111.4 jit_solution(11053210065946557868)
XLA Ops:
  1.3 0.8 select_reduce_fusion
  2.1 0.7 convert_element_type.17
  2.8 0.8 reshape.53.gain_ref
  3.6 0.1 copy.12.slot_col
  3.7 0.0 copy-start
  3.7 1.2 %copy-done = bf16[256,2048]{1,0:T(8,128)(2,1)S(1)} copy-done((bf16[256,2048]{1,0:T(8,128)(2,1)S(1)}, bf16[256,2048]{1,0:T(8,128)(2,1)}, u32[]{:S(2)}) %copy-start) | copy-done | bytes 1048600
  5.0 0.0 copy-start.1
  5.0 1.0 copy-done.1
  6.0 0.0 copy-start.2
  6.0 1.0 copy-done.2
  7.0 101.5 %shard_map.104 = (bf16[256,1024]{1,0:T(8,128)(2,1)S(1)}, bf16[256,256]{1,0:T(8,128)(2,1)S(1)}) custom-call(bf16[256,1024]{1,0:T(8,128)(2,1)S(1)} %copy-done.1, bf16[256,1024]{1,0:T(8,128)(2,1)S(1)} %copy-done.2, bf16[256,2048]{1,0:T(8,128)(2,1)S(1)} %copy-done, bf16[1024,2048]{1,0:T(8,128)(2,1)} %w_hbm.1, bf16[8192,256]{1,0:T(8,128)(2,1)} %cw_hbm.1, ...), custom_call_target="tpu_custom_call" | custom-call | flops 6000000000 | bytes 8000000 | tf_op jit(solution)/shard_map/pallas_call | solution.py:433
  108.5 0.1 fusion.12
  108.6 0.1 fusion.13
  108.7 1.9 %fusion.3 = bf16[256,256]{1,0:T(8,128)(2,1)} fusion(f32[256,1]{1,0:T(8,128)S(1)} %get-tuple-element.7, f32[256,255]{1,0:T(8,128)S(1)} %get-tuple-element.9, f32[256,255]{1,0:T(8,128)S(1)} %get-tuple-element.8, f32[256,1]{1,0:T(8,128)S(1)} %get-tuple-element.6, f32[256]{0:T(256)S(1)} %fusion.11, f32[256]{0:T(256)S(1)} %convert_element_type.17, ...), kind=kLoop, calls=%fused_computation.5 | loop fusion | flops 786432 | bytes 788992 | tf_op jit(solution)/shard_map/convert_element_type | solution.py:474
  110.6 0.8 copy.15
  (4 shorter events, 0.0 us)
Async XLA Ops:
  3.7 1.2 %copy-start = (bf16[256,2048]{1,0:T(8,128)(2,1)S(1)}, bf16[256,2048]{1,0:T(8,128)(2,1)}, u32[]{:S(2)}) copy-start(bf16[256,2048]{1,0:T(8,128)(2,1)} %kv_hbm.1) | copy-start | bytes 3145732
  5.0 1.0 copy-start.1
  6.0 1.0 copy-start.2

commit v2 on v1

--- a/solution.py
+++ b/solution.py
@@ -117,18 +117,21 @@
 
 
 def fused_kernel(
-    q_ref, r_ref, kv_hbm, w_hbm, cw_hbm, gain_ref, slot_row, slot_col,
+    q_hbm, r_hbm, kv_hbm, w_hbm, cw_hbm, gain_ref, keep_ref, count_ref,
     hid_out, cache_out,
-    kvbuf, w_ref, cw_ref, qown, qrecv, rown, rrecv, resbuf, attb, ownp, ysend, yrecv,
-    zsum, zrecv, hbuf, cmsg, crecv, cbuf, hpair,
+    q_ref, r_ref, kvbuf, w_ref, cw_ref, qown, qrecv, rown, rrecv, resbuf, attb, ownp, ysend, yrecv,
+    zsum, zrecv, hbuf, ymsg, ymsg_in, cmsg, crecv, cbuf, hpair,
     loc_sem, kv_s, kv_r, q_s, q_r, res_s, res_r, att_s, att_r, y_s, y_r, z_s, z_r,
-    ag_s, ag_r, ay_s, ay_r, c_s, c_r, row_s, row_r, fin_s, fin_r,
+    ag_s, ag_r, fw_s, ay_s, ay_r, cw_s, cw_r, c_s, c_r, row_s, row_r, fin_s, fin_r,
 ):
     c = lax.axis_index("ctx")
     t = lax.axis_index("tp")
     p, k = c // 2, c % 2
     z, y = t // 2, t % 2
     rows = q_ref.shape[0]
+    near = z + 1 - 2 * (z % 2)
+    cross = 2 - z // 2
+    is_inner = (z + 1) // 2 == 1
 
     def ctx_peer(i):
         return ((p + i // 2) % 2) * 2 + (k + i % 2) % 2
@@ -152,18 +155,21 @@
         pending.append(copy)
         return copy
 
-    w_copy = pltpu.make_async_copy(w_hbm, w_ref, loc_sem.at[0])
-    w_copy.start()
-    feat = cw_ref.shape[0]
-    cw_copy = pltpu.make_async_copy(
-        cw_hbm.at[pl.ds(pl.multiple_of(c * feat, feat), feat)], cw_ref, loc_sem.at[1]
-    )
-    cw_copy.start()
+    feat = cw_ref.shape[1]
     own_kv = kvbuf.at[pl.ds(pl.multiple_of(c * rows, rows), rows)]
     kv_copy = pltpu.make_async_copy(
         kv_hbm.at[:, pl.ds(pl.multiple_of(t * 2 * HD, 2 * HD), 2 * HD)], own_kv, loc_sem.at[2]
     )
     kv_copy.start()
+    q_load = pltpu.make_async_copy(q_hbm, q_ref, loc_sem.at[3])
+    q_load.start()
+    r_load = pltpu.make_async_copy(r_hbm, r_ref, loc_sem.at[4])
+    r_load.start()
+    w_copy = pltpu.make_async_copy(w_hbm, w_ref, loc_sem.at[0])
+    w_copy.start()
+    first_feat = pl.multiple_of((2 * c + y) * feat, feat)
+    cw_copy = pltpu.make_async_copy(cw_hbm.at[pl.ds(first_feat, feat)], cw_ref.at[0], loc_sem.at[1])
+    cw_copy.start()
 
     barrier = pltpu.get_barrier_semaphore()
     partners = [(ctx_peer(i), t) for i in (1, 2, 3)]
@@ -172,31 +178,52 @@
         pl.semaphore_signal(barrier, inc=1, device_id=dev, device_id_type=MESH)
     pl.semaphore_wait(barrier, len(partners))
 
-    slots = slot_row[...]
-    slot_at = lax.broadcasted_iota(jnp.int32, (KEPT, rows), 0)
-    pick_sib = jnp.where(slots == slot_at + (1 - k) * KEPT, 1.0, 0.0).astype(BF)
-    pick_own = jnp.where(slots == slot_at + k * KEPT, 1.0, 0.0).astype(BF)
+    count = count_ref[...]
+    base = jnp.where(k == 0, 0, 2 * KEPT - count)
+    chosen = keep_ref[...] == lax.broadcasted_iota(jnp.int32, (rows, rows), 0)
+    rank = lax.broadcasted_iota(jnp.int32, (rows, KEPT), 0)
+    slot_at = lax.broadcasted_iota(jnp.int32, (rows, KEPT), 1)
+    chosen = jnp.where(chosen, 1.0, 0.0).astype(BF)
+
+    def place_of(kk):
+        hit = (rank + base == slot_at + kk * KEPT) & (rank < count)
+        return jnp.dot(
+            chosen, jnp.where(hit, 1.0, 0.0).astype(BF), preferred_element_type=F32
+        ).astype(BF)
+
+    place_sib = place_of(1 - k)
+    place_own = place_of(k)
     row_id = lax.broadcasted_iota(jnp.int32, (rows, HD), 0).astype(F32)
     lane = lax.broadcasted_iota(jnp.int32, (rows, HD), 1)
     tags = jnp.where(lane == 0, row_id, jnp.where(lane == 1, 1.0, 0.0)).astype(BF)
     width = q_ref.shape[1]
 
     def pick(sel, what):
-        return jnp.dot(sel, what, preferred_element_type=F32).astype(BF)
+        return lax.dot_general(
+            sel, what, (((0,), (0,)), ((), ())), preferred_element_type=F32
+        ).astype(BF)
 
     kv_copy.wait()
-    kv_copies = [
-        send(own_kv, own_kv, kv_s.at[i - 1], kv_r.at[i - 1], (ctx_peer(i), t)) for i in (2, 3, 1)
-    ]
-    qown[0, :, :width] = pick(pick_sib, q_ref[...])
-    qown[0, :, width:] = pick(pick_sib, tags)
+    kv_far = send(own_kv, own_kv, kv_s.at[0], kv_r.at[0], (ctx_peer(2), t))
+    kv_sib = send(own_kv, own_kv, kv_s.at[1], kv_r.at[1], (sib, t))
+    cw_send = send(
+        cw_hbm.at[pl.ds(pl.multiple_of((2 * c + 1 - y) * feat, feat), feat)],
+        cw_ref.at[1], cw_s, cw_r, ydev,
+    )
+    q_load.wait()
+    qown[0, :, :width] = pick(place_sib, q_ref[...])
+    qown[0, :, width:] = pick(place_sib, tags)
     q_copy = send(qown.at[0], qrecv, q_s.at[0], q_r.at[0], (sib, t))
-    rown[0] = pick(pick_sib, r_ref[...])
+    r_load.wait()
+    rown[0] = pick(place_sib, r_ref[...])
     r_copy = send(rown.at[0], rrecv, q_s.at[1], q_r.at[1], (sib, t))
-    qown[1, :, :width] = pick(pick_own, q_ref[...])
-    qown[1, :, width:] = pick(pick_own, tags)
-    rown[1] = pick(pick_own, r_ref[...])
-
+    qown[1, :, :width] = pick(place_own, q_ref[...])
+    qown[1, :, width:] = pick(place_own, tags)
+    rown[1] = pick(place_own, r_ref[...])
+
+    kv_far.wait_recv()
+    far_kv = kvbuf.at[pl.ds(pl.multiple_of(ctx_peer(2) * rows, rows), rows)]
+    kv_diag = send(far_kv, far_kv, kv_s.at[2], kv_r.at[2], (sib, t))
     q_copy.wait_recv()
     own_tag = qown[1, :, width:].astype(F32)
     sib_tag = qrecv[:, width:].astype(F32)
@@ -222,8 +249,8 @@
     def _():
         res_copy.start()
 
-    for copy in kv_copies:
-        copy.wait_recv()
+    kv_sib.wait_recv()
+    kv_diag.wait_recv()
     total = kvbuf.shape[0]
     col_id = lax.broadcasted_iota(jnp.int32, (KEPT, total), 1).astype(F32)
     seen = col_id <= limit
@@ -237,7 +264,7 @@
         ) * scale
         s = jnp.where(seen, s, -1e30)
         top = jnp.max(s, axis=1, keepdims=True)
-        e = jnp.where(seen, jnp.exp(s - top), 0.0)
+        e = jnp.exp(s - top)
         den = jnp.sum(e, axis=1, keepdims=True)
         mixed = jnp.dot(e.astype(BF), values, preferred_element_type=F32)
         attb[0, :, cols] = (mixed / den).astype(BF)
@@ -289,52 +316,83 @@
         hid = zsum[i, z].astype(F32)
         for d in range(Z - 1):
             hid = hid + zrecv[i, d].astype(F32)
-        hbuf[i, y, z] = hid.astype(BF)
-        for d in (2, 1, 3):
-            ags[i, d] = send(
-                hbuf.at[i, y, z], hbuf.at[i, y, z], ag_s.at[i, d - 1], ag_r.at[i, d - 1],
-                (c, z_peer(d) * 2 + y),
-            )
+        hbuf[i, z] = hid.astype(BF)
+        piece = hbuf.at[i, z]
+        ags[i, 0] = send(piece, piece, ag_s.at[i, 0], ag_r.at[i, z], (c, cross * 2 + y))
+        ags[i, 1] = send(piece, piece, ag_s.at[i, 1], ag_r.at[i, z], (c, near * 2 + y))
+
+    def piece_copy(i, zz):
+        piece = hbuf.at[i, zz]
+        return remote(piece, piece, fw_s.at[i, zz % 2], ag_r.at[i, zz], (c, near * 2 + y))
+
+    other = 2 * (1 - z // 2)
+
+    def stage_f(i):
+        @pl.when(is_inner)
+        def _():
+            for j in range(2):
+                piece_copy(i, other + j).wait_recv()
+                piece_copy(i, other + j).start()
 
     def row_copy(i):
         return remote(
-            hbuf.at[i, y], hpair.at[(k + i % 2) % 2], row_s.at[i], row_r, (ctx_peer(i), t)
+            hbuf.at[i], hpair.at[(k + i % 2) % 2], row_s.at[i], row_r, (ctx_peer(i), t)
         )
 
+    own_part = {}
+
+    def packed(acc, squares):
+        coarse = squares.astype(BF).astype(F32)
+        at = lax.broadcasted_iota(jnp.int32, (KEPT, HD), 1)
+        tail = jnp.where(at == 0, coarse, jnp.where(at == 1, squares - coarse, 0.0))
+        return acc.astype(BF), tail.astype(BF)
+
+    def unpacked(ref, i):
+        tail = ref[i, :, 256:].astype(F32)
+        return ref[i, :, :256].astype(F32), tail[:, 0:1] + tail[:, 1:2]
+
     def stage_d(i):
-        for d in (1, 2, 3):
-            ags[i, d].wait_recv()
-        ays[i] = send(hbuf.at[i, y], hbuf.at[i, y], ay_s.at[i], ay_r.at[i], ydev)
+        piece_copy(i, near).wait_recv()
+
+        @pl.when(jnp.logical_not(is_inner))
+        def _():
+            for j in range(2):
+                piece_copy(i, other + j).wait_recv()
 
         @pl.when(is_root)
         def _():
             if i == 0:
-                hpair[k] = hbuf[i, y]
+                hpair[k] = hbuf[i]
             else:
                 row_copy(i).start()
 
-    gains = gain_ref[c]
+        if i == 0:
+            cw_copy.wait()
+            cw_send.wait_recv()
+        far = jnp.zeros((KEPT, 256), F32)
+        acc = jnp.zeros((KEPT, 256), F32)
+        squares = jnp.zeros((KEPT, 1), F32)
+        for q in range(Z):
+            wide = hbuf[i, q].astype(F32)
+            squares = squares + jnp.sum(wide * wide, axis=1, keepdims=True)
+            gain = gain_ref[:, pl.ds(pl.multiple_of(first_feat + q * 256, 256), 256)]
+            scaled = (wide * gain).astype(BF)
+            cut = slice(q * 256, (q + 1) * 256)
+            far = far + jnp.dot(scaled, cw_ref[1, cut], preferred_element_type=F32)
+            acc = acc + jnp.dot(scaled, cw_ref[0, cut], preferred_element_type=F32)
+        ymsg[i, :, :256], ymsg[i, :, 256:] = packed(far, squares)
+        ays[i] = send(ymsg.at[i], ymsg_in.at[i], ay_s.at[i], ay_r.at[i], ydev)
+        own_part[i] = acc, squares
 
     def stage_e(i):
         ays[i].wait_recv()
-        acc = jnp.zeros((KEPT, 256), F32)
-        squares = jnp.zeros((KEPT, 1), F32)
-        for q in range(2 * Z):
-            wide = hbuf[i, q // Z, q % Z].astype(F32)
-            squares = squares + jnp.sum(wide * wide, axis=1, keepdims=True)
-            acc = acc + jnp.dot(
-                (wide * gains[q : q + 1, :]).astype(BF),
-                cw_ref[q * 256 : (q + 1) * 256, :],
-                preferred_element_type=F32,
-            )
+        acc, squares = own_part[i]
+        more, more_squares = unpacked(ymsg_in, i)
+        acc = acc + more
+        squares = squares + more_squares
         if i == 0:
             return acc, squares
-        coarse = squares.astype(BF).astype(F32)
-        at = lax.broadcasted_iota(jnp.int32, (KEPT, HD), 1)
-        cmsg[i - 1, :, :256] = acc.astype(BF)
-        cmsg[i - 1, :, 256:] = jnp.where(
-            at == 0, coarse, jnp.where(at == 1, squares - coarse, 0.0)
-        ).astype(BF)
+        cmsg[i - 1, :, :256], cmsg[i - 1, :, 256:] = packed(acc, squares)
         cs[i] = send(
             cmsg.at[i - 1], crecv.at[i - 1], c_s.at[i - 1], c_r.at[i - 1], (ctx_peer(i), t)
         )
@@ -349,13 +407,15 @@
     stage_a(3)
     stage_b(2)
     stage_c(1)
-    stage_d(0)
+    stage_f(0)
     stage_b(3)
     stage_c(2)
+    stage_f(1)
+    stage_d(0)
+    stage_c(3)
+    stage_f(2)
     stage_d(1)
-    cw_copy.wait()
-    acc, squares = stage_e(0)
-    stage_c(3)
+    stage_f(3)
     stage_d(2)
     stage_e(1)
     stage_d(3)
@@ -367,9 +427,8 @@
 
     pair_copy = send(hpair.at[k], hpair.at[k], fin_s.at[0], fin_r.at[0], (sib, t))
     stage_e(3)
-    slots_c = slot_col[...]
-    place_at = lax.broadcasted_iota(jnp.int32, (rows, KEPT), 1)
-    place = [jnp.where(slots_c == place_at + kk * KEPT, 1.0, 0.0).astype(BF) for kk in range(2)]
+    acc, squares = stage_e(0)
+    place = [place_of(kk) for kk in range(2)]
     pair_copy.wait_recv()
     for j in range(Z):
         hid_out[:, j * 256 : (j + 1) * 256] = (
@@ -378,9 +437,9 @@
         ).astype(BF)
     for i in (1, 2, 3):
         cs[i].wait_recv()
-        got = crecv[i - 1, :, 256:].astype(F32)
-        acc = acc + crecv[i - 1, :, :256].astype(F32)
-        squares = squares + got[:, 0:1] + got[:, 1:2]
+        more, more_squares = unpacked(crecv, i - 1)
+        acc = acc + more
+        squares = squares + more_squares
     cbuf[k] = (acc * lax.rsqrt(squares / D + EPS)).astype(BF)
     last = send(cbuf.at[k], cbuf.at[k], fin_s.at[1], fin_r.at[1], (sib, t))
     last.wait_recv()
@@ -400,6 +459,12 @@
     def _():
         for i in (1, 2, 3):
             row_copy(i).wait_send()
+
+    @pl.when(is_inner)
+    def _():
+        for i in range(4):
+            for j in range(2):
+                piece_copy(i, other + j).wait_send()
 
 
 def rotate_head(raw, position_ids):
@@ -419,12 +484,6 @@
     residual, queries, keys_values, out_weight, norm_gain, cache_weight, positions, keep_rows, kept_count
 ):
     rows, width = queries.shape
-    ctx_index = lax.axis_index("ctx")
-    own_count = kept_count[0]
-    base = jnp.where(ctx_index % 2 == 0, 0, 2 * KEPT - own_count)
-    order = jnp.arange(rows, dtype=jnp.int32)
-    at = jnp.where(order < own_count, base + order + 1, 0)
-    slot = jnp.sum(jnp.where(keep_rows[None, :] == order[:, None], at[None, :], 0), axis=1) - 1
     feat = out_weight.shape[1]
     n_ctx = D // feat
     dma = pltpu.SemaphoreType.DMA
@@ -436,12 +495,14 @@
             jax.ShapeDtypeStruct((rows, width), BF),
             jax.ShapeDtypeStruct((rows, 2 * HD), BF),
         ),
-        in_specs=[vmem, vmem, hbm, hbm, hbm, vmem, vmem, vmem],
+        in_specs=[hbm, hbm, hbm, hbm, hbm, vmem, vmem, vmem],
         out_specs=(vmem, vmem),
         scratch_shapes=[
+            pltpu.VMEM((rows, width), BF),
+            pltpu.VMEM((rows, width), BF),
             pltpu.VMEM((n_ctx * rows, 2 * HD), BF),
             pltpu.VMEM(out_weight.shape, BF),
-            pltpu.VMEM((feat, 2 * HD), BF),
+            pltpu.VMEM((2, feat // 2, 2 * HD), BF),
             pltpu.VMEM((2, KEPT, width + HD), BF),
             pltpu.VMEM((KEPT, width + HD), BF),
             pltpu.VMEM((2, KEPT, width), BF),
@@ -453,14 +514,16 @@
             pltpu.VMEM((4, KEPT, width), BF),
             pltpu.VMEM((4, Z, KEPT, 256), BF),
             pltpu.VMEM((4, Z - 1, KEPT, 256), BF),
-            pltpu.VMEM((4, 2, Z, KEPT, 256), BF),
+            pltpu.VMEM((4, Z, KEPT, 256), BF),
+            pltpu.VMEM((4, KEPT, 256 + HD), BF),
+            pltpu.VMEM((4, KEPT, 256 + HD), BF),
             pltpu.VMEM((3, KEPT, 256 + HD), BF),
             pltpu.VMEM((3, KEPT, 256 + HD), BF),
             pltpu.VMEM((2, KEPT, 256), BF),
             pltpu.VMEM((2, Z, KEPT, 256), BF),
-            dma((3,)), dma((3,)), dma((3,)), dma((2,)), dma((2,)), dma, dma((4,)),
+            dma((5,)), dma((3,)), dma((3,)), dma((2,)), dma((2,)), dma, dma((4,)),
             dma((3,)), dma((3,)), dma((4,)), dma((4,)), dma((4, 3)), dma((4, 3)),
-            dma((4, 3)), dma((4, 3)), dma((4,)), dma((4,)), dma((3,)), dma((3,)),
+            dma((4, 2)), dma((4, 4)), dma((4, 2)), dma((4,)), dma((4,)), dma, dma, dma((3,)), dma((3,)),
             dma((4,)), dma, dma((2,)), dma((2,)),
         ],
         compiler_params=pltpu.CompilerParams(
@@ -469,7 +532,7 @@
         cost_estimate=pl.CostEstimate(flops=6_000_000_000, bytes_accessed=8_000_000, transcendentals=1_400_000),
     )(
         queries, residual, keys_values, out_weight, cache_weight,
-        norm_gain.reshape(n_ctx, feat // 256, 256), slot[None, :], slot[:, None],
+        norm_gain[None, :], keep_rows[None, :], kept_count[None, :],
     )
     kept_cache = rotate_head(raw.astype(F32), positions).astype(BF)
     return (kept_hidden, kept_cache)

time: 112 us -> 100 us (0.89)
  Pallas kernels: 101 us -> 90.1 us
    pallas_call x1, Pallas kernels: 101 us -> 90.1 us  [fused_shards(): pl.pallas_call(fused_kernel, out_shape=(jax.ShapeDtypeStruct((rows, width...]
    unnamed x7 -> x11, local copies, waits for them, and re-layouts: 4.1 us -> 5.53 us
where the time goes in v2:
time: 100 us; the launch traced here: 99.7 us
  Pallas kernels  90.1 us (90%)
  local copies, waits for them, and re-layouts  5.73 us (6%)
  other arithmetic  2.57 us (3%)
  between operations  1.3 us (1%)
    pallas_call x1, Pallas kernels, fused_shards(): pl.pallas_call(fused_kernel, out_shape=(jax.ShapeDtypeStruct((rows, width...  90.1 us
    unnamed x11, local copies, waits for them, and re-layouts  5.53 us

profile of v2, /device:TPU:0, one launch (start us, length us, event | category | flops | bytes accessed | tf_op | source)
XLA Modules:
  0.0 99.7 jit_solution(3173425046116326658)
XLA Ops:
  1.3 0.7 convert_element_type.17
  2.0 0.0 copy-start
  2.0 1.2 %copy-done = bf16[256,2048]{1,0:T(8,128)(2,1)S(1)} copy-done((bf16[256,2048]{1,0:T(8,128)(2,1)S(1)}, bf16[256,2048]{1,0:T(8,128)(2,1)}, u32[]{:S(2)}) %copy-start) | copy-done | bytes 1048600
  3.2 0.0 copy-start.1
  3.2 1.0 %copy-done.1 = bf16[256,1024]{1,0:T(8,128)(2,1)S(1)} copy-done((bf16[256,1024]{1,0:T(8,128)(2,1)S(1)}, bf16[256,1024]{1,0:T(8,128)(2,1)}, u32[]{:S(2)}) %copy-start.1) | copy-done | bytes 524312
  4.2 0.0 copy-start.2
  4.2 1.0 %copy-done.2 = bf16[256,1024]{1,0:T(8,128)(2,1)S(1)} copy-done((bf16[256,1024]{1,0:T(8,128)(2,1)S(1)}, bf16[256,1024]{1,0:T(8,128)(2,1)}, u32[]{:S(2)}) %copy-start.2) | copy-done | bytes 524312
  5.3 0.0 copy-start.3
  5.3 0.8 copy-done.3
  6.0 0.0 copy-start.4
  6.1 0.7 copy-done.4
  6.7 90.1 %shard_map.104 = (bf16[256,1024]{1,0:T(8,128)(2,1)S(1)}, bf16[256,256]{1,0:T(8,128)(2,1)S(1)}) custom-call(bf16[256,1024]{1,0:T(8,128)(2,1)S(1)} %copy-done.1, bf16[256,1024]{1,0:T(8,128)(2,1)S(1)} %copy-done.2, bf16[256,2048]{1,0:T(8,128)(2,1)S(1)} %copy-done, bf16[1024,2048]{1,0:T(8,128)(2,1)} %w_hbm.1, bf16[8192,256]{1,0:T(8,128)(2,1)} %cw_hbm.1, ...), custom_call_target="tpu_custom_call" | custom-call | flops 6000000000 | bytes 8000000 | tf_op jit(solution)/shard_map/pallas_call | solution.py:492
  96.8 0.1 fusion.12
  96.9 0.1 fusion.13
  97.0 1.9 %fusion.3 = bf16[256,256]{1,0:T(8,128)(2,1)} fusion(f32[256,1]{1,0:T(8,128)S(1)} %get-tuple-element.7, f32[256,255]{1,0:T(8,128)S(1)} %get-tuple-element.9, f32[256,255]{1,0:T(8,128)S(1)} %get-tuple-element.8, f32[256,1]{1,0:T(8,128)S(1)} %get-tuple-element.6, f32[256]{0:T(256)S(1)} %fusion.11, f32[256]{0:T(256)S(1)} %convert_element_type.17, ...), kind=kLoop, calls=%fused_computation.5 | loop fusion | flops 786432 | bytes 788992 | tf_op jit(solution)/shard_map/convert_element_type | solution.py:537
  98.9 0.8 copy.13
  (2 shorter events, 0.0 us)
Async XLA Ops:
  2.0 1.2 %copy-start = (bf16[256,2048]{1,0:T(8,128)(2,1)S(1)}, bf16[256,2048]{1,0:T(8,128)(2,1)}, u32[]{:S(2)}) copy-start(bf16[256,2048]{1,0:T(8,128)(2,1)} %kv_hbm.1) | copy-start | bytes 3145732
  3.2 1.0 %copy-start.1 = (bf16[256,1024]{1,0:T(8,128)(2,1)S(1)}, bf16[256,1024]{1,0:T(8,128)(2,1)}, u32[]{:S(2)}) copy-start(bf16[256,1024]{1,0:T(8,128)(2,1)} %q_hbm.1) | copy-start | bytes 1572868
  4.2 1.0 %copy-start.2 = (bf16[256,1024]{1,0:T(8,128)(2,1)S(1)}, bf16[256,1024]{1,0:T(8,128)(2,1)}, u32[]{:S(2)}) copy-start(bf16[256,1024]{1,0:T(8,128)(2,1)} %r_hbm.1) | copy-start | bytes 1572868
  5.3 0.8 copy-start.3
  6.0 0.7 copy-start.4

commit v3 on v2

--- a/solution.py
+++ b/solution.py
@@ -117,11 +117,11 @@
 
 
 def fused_kernel(
-    q_hbm, r_hbm, kv_hbm, w_hbm, cw_hbm, gain_ref, keep_ref, count_ref,
+    q_hbm, r_hbm, kv_hbm, w_hbm, cw_hbm, gain_hbm, keep_hbm, count_ref,
     hid_out, cache_out,
-    q_ref, r_ref, kvbuf, w_ref, cw_ref, qown, qrecv, rown, rrecv, resbuf, attb, ownp, ysend, yrecv,
-    zsum, zrecv, hbuf, ymsg, ymsg_in, cmsg, crecv, cbuf, hpair,
-    loc_sem, kv_s, kv_r, q_s, q_r, res_s, res_r, att_s, att_r, y_s, y_r, z_s, z_r,
+    gain_ref, keep_ref, q_ref, r_ref, kvbuf, w_ref, cw_ref, qown, qrecv, rown, rrecv, resbuf, attb, ownp, ysend, yrecv,
+    zsum, zrecv, xrecv, hbuf, ymsg, ymsg_in, cmsg, crecv, cbuf, hpair,
+    loc_sem, kv_s, kv_r, q_s, q_r, res_s, res_r, att_s, att_r, y_s, y_r, z_s, z_r, x_r,
     ag_s, ag_r, fw_s, ay_s, ay_r, cw_s, cw_r, c_s, c_r, row_s, row_r, fin_s, fin_r,
 ):
     c = lax.axis_index("ctx")
@@ -130,14 +130,11 @@
     z, y = t // 2, t % 2
     rows = q_ref.shape[0]
     near = z + 1 - 2 * (z % 2)
-    cross = 2 - z // 2
+    cross = Z - 1 - z
     is_inner = (z + 1) // 2 == 1
 
     def ctx_peer(i):
         return ((p + i // 2) % 2) * 2 + (k + i % 2) % 2
-
-    def z_peer(d):
-        return (z + d) % Z
 
     sib = ctx_peer(1)
     ydev = (c, 2 * z + 1 - y)
@@ -161,6 +158,8 @@
         kv_hbm.at[:, pl.ds(pl.multiple_of(t * 2 * HD, 2 * HD), 2 * HD)], own_kv, loc_sem.at[2]
     )
     kv_copy.start()
+    keep_load = pltpu.make_async_copy(keep_hbm, keep_ref, loc_sem.at[5])
+    keep_load.start()
     q_load = pltpu.make_async_copy(q_hbm, q_ref, loc_sem.at[3])
     q_load.start()
     r_load = pltpu.make_async_copy(r_hbm, r_ref, loc_sem.at[4])
@@ -171,14 +170,18 @@
     cw_copy = pltpu.make_async_copy(cw_hbm.at[pl.ds(first_feat, feat)], cw_ref.at[0], loc_sem.at[1])
     cw_copy.start()
 
+    gain_load = pltpu.make_async_copy(gain_hbm, gain_ref, loc_sem.at[6])
+    gain_load.start()
+
     barrier = pltpu.get_barrier_semaphore()
     partners = [(ctx_peer(i), t) for i in (1, 2, 3)]
-    partners += [(c, z_peer(d) * 2 + y) for d in (1, 2, 3)] + [ydev]
+    partners += [(c, zz * 2 + y) for zz in (near, cross)] + [ydev]
     for dev in partners:
         pl.semaphore_signal(barrier, inc=1, device_id=dev, device_id_type=MESH)
     pl.semaphore_wait(barrier, len(partners))
 
     count = count_ref[...]
+    keep_load.wait()
     base = jnp.where(k == 0, 0, 2 * KEPT - count)
     chosen = keep_ref[...] == lax.broadcasted_iota(jnp.int32, (rows, rows), 0)
     rank = lax.broadcasted_iota(jnp.int32, (rows, KEPT), 0)
@@ -272,11 +275,27 @@
     att_cp = send(attb.at[0], attb.at[2], att_s.at[0], att_r.at[0], (ctx_peer(2), t))
     att_sib = send(attb.at[0], attb.at[1], att_s.at[1], att_r.at[1], (sib, t))
     half = Z * 256
-    own_cols = pl.ds(pl.multiple_of(y * half, half), half)
-    far_cols = pl.ds(pl.multiple_of((1 - y) * half, half), half)
+    other = 2 * (1 - z // 2)
+    mine = 2 - other
+    is_outer = jnp.logical_not(is_inner)
+    near_dev = (c, near * 2 + y)
+    cross_dev = (c, cross * 2 + y)
+    sequence = [(jj, other + jj) for jj in range(2)] + [(2 + jj, mine + jj) for jj in range(2)]
+
+    def piece_of(who, j):
+        return pl.ds(pl.multiple_of(who * half + j * 256, 256), 256)
+
+    def y_copy(i, j):
+        return remote(ysend.at[i, j], yrecv.at[i, j], y_s.at[i, j], y_r.at[i, j], ydev)
+
+    def out_copy(i, j):
+        return remote(zsum.at[i, j], zrecv.at[i, j], z_s.at[i, j], z_r.at[i, j], near_dev)
+
+    def cross_copy(i, j):
+        return remote(zsum.at[i, j], xrecv.at[i, j], z_s.at[i, j], x_r.at[i, j], cross_dev)
     w_copy.wait()
     fwd = {}
-    ys, zs, ags, ays, cs = {}, {}, {}, {}, {}
+    ays, cs = {}, {}
 
     def stage_a(i):
         if i == 1:
@@ -286,53 +305,72 @@
             fwd[0] = send(attb.at[2], attb.at[3], att_s.at[2], att_r.at[2], (sib, t))
         if i == 3:
             fwd[0].wait_recv()
-        ysend[i] = jnp.dot(attb[i], w_ref[:, far_cols], preferred_element_type=F32).astype(BF)
-        ys[i] = send(ysend.at[i], yrecv.at[i], y_s.at[i], y_r.at[i], ydev)
-        ownp[i] = jnp.dot(attb[i], w_ref[:, own_cols], preferred_element_type=F32)
+        for _, j in sequence:
+            ysend[i, j] = jnp.dot(
+                attb[i], w_ref[:, piece_of(1 - y, j)], preferred_element_type=F32
+            ).astype(BF)
+            copy = y_copy(i, j)
+            copy.start()
+            pending.append(copy)
+        for _, j in sequence:
+            ownp[i, j] = jnp.dot(
+                attb[i], w_ref[:, piece_of(y, j)], preferred_element_type=F32
+            )
 
     def stage_b(i):
-        ys[i].wait_recv()
-
         @pl.when(is_root)
         def _():
             if i > 0:
                 remote(
                     rown.at[1], resbuf.at[i], res_s, res_r.at[i], (ctx_peer(i), t)
                 ).wait_recv()
-            ownp[i] = ownp[i] + resbuf[i].astype(F32)
-
-        for j in range(Z):
-            cols = slice(j * 256, (j + 1) * 256)
-            zsum[i, j] = (ownp[i, :, cols] + yrecv[i, :, cols].astype(F32)).astype(BF)
-        for d in (2, 1, 3):
-            zs[i, d] = send(
-                zsum.at[i, z_peer(d)], zrecv.at[i, d - 1], z_s.at[i, d - 1], z_r.at[i, d - 1],
-                (c, z_peer(d) * 2 + y),
-            )
+            for j in range(Z):
+                ownp[i, j] = ownp[i, j] + resbuf[i, :, j * 256 : (j + 1) * 256].astype(F32)
+
+        for _, j in sequence:
+            y_copy(i, j).wait_recv()
+            total = ownp[i, j] + yrecv[i, j].astype(F32)
+
+            @pl.when(is_outer)
+            def _():
+                zsum[i, j] = total.astype(BF)
+                out_copy(i, j).start()
+
+            @pl.when(is_inner)
+            def _():
+                ownp[i, j] = total
+
+    def stage_g(i):
+        @pl.when(is_inner)
+        def _():
+            for n, j in sequence:
+                out_copy(i, j).wait_recv()
+                total = ownp[i, j] + zrecv[i, j].astype(F32)
+                if n < 2:
+                    zsum[i, j] = total.astype(BF)
+                    cross_copy(i, j).start()
+                else:
+                    ownp[i, j] = total
+
+    def piece_copy(i, j, dev, sem):
+        piece = hbuf.at[i, j]
+        return remote(piece, piece, sem.at[i, j], ag_r.at[i, j], dev)
 
     def stage_c(i):
-        for d in (1, 2, 3):
-            zs[i, d].wait_recv()
-        hid = zsum[i, z].astype(F32)
-        for d in range(Z - 1):
-            hid = hid + zrecv[i, d].astype(F32)
-        hbuf[i, z] = hid.astype(BF)
-        piece = hbuf.at[i, z]
-        ags[i, 0] = send(piece, piece, ag_s.at[i, 0], ag_r.at[i, z], (c, cross * 2 + y))
-        ags[i, 1] = send(piece, piece, ag_s.at[i, 1], ag_r.at[i, z], (c, near * 2 + y))
-
-    def piece_copy(i, zz):
-        piece = hbuf.at[i, zz]
-        return remote(piece, piece, fw_s.at[i, zz % 2], ag_r.at[i, zz], (c, near * 2 + y))
-
-    other = 2 * (1 - z // 2)
+        @pl.when(is_inner)
+        def _():
+            for n, j in sequence[2:]:
+                cross_copy(i, j).wait_recv()
+                hbuf[i, j] = (ownp[i, j] + xrecv[i, j].astype(F32)).astype(BF)
+                piece_copy(i, j, cross_dev, ag_s).start()
+                piece_copy(i, j, near_dev, fw_s).start()
 
     def stage_f(i):
         @pl.when(is_inner)
         def _():
-            for j in range(2):
-                piece_copy(i, other + j).wait_recv()
-                piece_copy(i, other + j).start()
+            for n, j in sequence[:2]:
+                piece_copy(i, j, cross_dev, ag_s).wait_recv()
+                piece_copy(i, j, near_dev, fw_s).start()
 
     def row_copy(i):
         return remote(
@@ -352,12 +390,10 @@
         return ref[i, :, :256].astype(F32), tail[:, 0:1] + tail[:, 1:2]
 
     def stage_d(i):
-        piece_copy(i, near).wait_recv()
-
-        @pl.when(jnp.logical_not(is_inner))
+        @pl.when(is_outer)
         def _():
-            for j in range(2):
-                piece_copy(i, other + j).wait_recv()
+            for _, j in sequence[2:] + sequence[:2]:
+                piece_copy(i, j, near_dev, fw_s).wait_recv()
 
         @pl.when(is_root)
         def _():
@@ -367,6 +403,7 @@
                 row_copy(i).start()
 
         if i == 0:
+            gain_load.wait()
             cw_copy.wait()
             cw_send.wait_recv()
         far = jnp.zeros((KEPT, 256), F32)
@@ -403,12 +440,16 @@
     stage_b(0)
     stage_a(2)
     stage_b(1)
-    stage_c(0)
+    stage_g(0)
     stage_a(3)
     stage_b(2)
+    stage_g(1)
+    stage_c(0)
+    stage_b(3)
+    stage_g(2)
     stage_c(1)
     stage_f(0)
-    stage_b(3)
+    stage_g(3)
     stage_c(2)
     stage_f(1)
     stage_d(0)
@@ -463,8 +504,18 @@
     @pl.when(is_inner)
     def _():
         for i in range(4):
-            for j in range(2):
-                piece_copy(i, other + j).wait_send()
+            for n, j in sequence:
+                piece_copy(i, j, near_dev, fw_s).wait_send()
+                if n < 2:
+                    cross_copy(i, j).wait_send()
+                else:
+                    piece_copy(i, j, cross_dev, ag_s).wait_send()
+
+    @pl.when(is_outer)
+    def _():
+        for i in range(4):
+            for _, j in sequence:
+                out_copy(i, j).wait_send()
 
 
 def rotate_head(raw, position_ids):
@@ -495,9 +546,11 @@
             jax.ShapeDtypeStruct((rows, width), BF),
             jax.ShapeDtypeStruct((rows, 2 * HD), BF),
         ),
-        in_specs=[hbm, hbm, hbm, hbm, hbm, vmem, vmem, vmem],
+        in_specs=[hbm] * 7 + [vmem],
         out_specs=(vmem, vmem),
         scratch_shapes=[
+            pltpu.VMEM((1, D), F32),
+            pltpu.VMEM((1, rows), jnp.int32),
             pltpu.VMEM((rows, width), BF),
             pltpu.VMEM((rows, width), BF),
             pltpu.VMEM((n_ctx * rows, 2 * HD), BF),
@@ -509,11 +562,12 @@
             pltpu.VMEM((KEPT, width), BF),
             pltpu.VMEM((4, KEPT, width), BF),
             pltpu.VMEM((4, KEPT, width), BF),
-            pltpu.VMEM((4, KEPT, width), F32),
-            pltpu.VMEM((4, KEPT, width), BF),
-            pltpu.VMEM((4, KEPT, width), BF),
+            pltpu.VMEM((4, Z, KEPT, 256), F32),
             pltpu.VMEM((4, Z, KEPT, 256), BF),
-            pltpu.VMEM((4, Z - 1, KEPT, 256), BF),
+            pltpu.VMEM((4, Z, KEPT, 256), BF),
+            pltpu.VMEM((4, Z, KEPT, 256), BF),
+            pltpu.VMEM((4, Z, KEPT, 256), BF),
+            pltpu.VMEM((4, Z, KEPT, 256), BF),
             pltpu.VMEM((4, Z, KEPT, 256), BF),
             pltpu.VMEM((4, KEPT, 256 + HD), BF),
             pltpu.VMEM((4, KEPT, 256 + HD), BF),
@@ -521,13 +575,13 @@
             pltpu.VMEM((3, KEPT, 256 + HD), BF),
             pltpu.VMEM((2, KEPT, 256), BF),
             pltpu.VMEM((2, Z, KEPT, 256), BF),
-            dma((5,)), dma((3,)), dma((3,)), dma((2,)), dma((2,)), dma, dma((4,)),
-            dma((3,)), dma((3,)), dma((4,)), dma((4,)), dma((4, 3)), dma((4, 3)),
-            dma((4, 2)), dma((4, 4)), dma((4, 2)), dma((4,)), dma((4,)), dma, dma, dma((3,)), dma((3,)),
+            dma((7,)), dma((3,)), dma((3,)), dma((2,)), dma((2,)), dma, dma((4,)),
+            dma((3,)), dma((3,)), dma((4, 4)), dma((4, 4)), dma((4, 4)), dma((4, 4)), dma((4, 4)),
+            dma((4, 4)), dma((4, 4)), dma((4, 4)), dma((4,)), dma((4,)), dma, dma, dma((3,)), dma((3,)),
             dma((4,)), dma, dma((2,)), dma((2,)),
         ],
         compiler_params=pltpu.CompilerParams(
-            collective_id=0, has_side_effects=True, vmem_limit_bytes=48 * 1024 * 1024
+            collective_id=0, has_side_effects=True, vmem_limit_bytes=60 * 1024 * 1024
         ),
         cost_estimate=pl.CostEstimate(flops=6_000_000_000, bytes_accessed=8_000_000, transcendentals=1_400_000),
     )(

time: 100 us -> 97.9 us (0.979)
  local copies, waits for them, and re-layouts: 5.73 us -> 3.92 us
  Pallas kernels: 90.1 us -> 88.7 us
    unnamed x11 -> x1, local copies, waits for them, and re-layouts: 5.53 us -> 1.87 us
    slice x2, local copies, waits for them, and re-layouts: 0.2 us -> 2.05 us  [rotate_head(): jnp.roll(raw, 1, axis=1)]
    pallas_call x1, Pallas kernels: 90.1 us -> 88.7 us  [fused_shards(): pl.pallas_call(fused_kernel, out_shape=(jax.ShapeDtypeStruct((rows, width...]
where the time goes in v3:
time: 97.9 us; the launch traced here: 97.3 us
  Pallas kernels  88.7 us (91%)
  local copies, waits for them, and re-layouts  3.92 us (4%)
  other arithmetic  3.39 us (3%)
  between operations  1.29 us (1%)
    pallas_call x1, Pallas kernels, fused_shards(): pl.pallas_call(fused_kernel, out_shape=(jax.ShapeDtypeStruct((rows, width...  88.7 us
    convert_element_type x1, other arithmetic, fused_shards(): kept_cache = rotate_head(raw.astype(F32), positions).astype(BF)  2.7 us
    slice x2, local copies, waits for them, and re-layouts, rotate_head(): jnp.roll(raw, 1, axis=1)  2.05 us

profile of v3, /device:TPU:0, one launch (start us, length us, event | category | flops | bytes accessed | tf_op | source)
XLA Modules:
  0.0 97.3 jit_solution(9272353190480118046)
XLA Ops:
  1.3 0.7 convert_element_type.17
  2.0 88.7 %shard_map.104 = (bf16[256,1024]{1,0:T(8,128)(2,1)}, bf16[256,256]{1,0:T(8,128)(2,1)}) custom-call(bf16[256,1024]{1,0:T(8,128)(2,1)} %q_hbm.1, bf16[256,1024]{1,0:T(8,128)(2,1)} %r_hbm.1, bf16[256,2048]{1,0:T(8,128)(2,1)} %kv_hbm.1, bf16[1024,2048]{1,0:T(8,128)(2,1)} %w_hbm.1, bf16[8192,256]{1,0:T(8,128)(2,1)} %cw_hbm.1, f32[1,8192]{1,0:T(1,128)} %bitcast.4, ...), custom_call_target="tpu_custom_call" | custom-call | flops 6000000000 | bytes 8000000 | tf_op jit(solution)/shard_map/pallas_call | solution.py:543
  90.7 1.0 fusion.12
  91.7 1.1 %fusion.13 = (f32[256,255]{1,0:T(8,128)S(1)}, f32[256,255]{1,0:T(8,128)S(1)}) fusion(bf16[256,256]{1,0:T(8,128)(2,1)} %get-tuple-element.5), kind=kLoop, calls=%fused_computation.21 | loop fusion | bytes 1044480 | tf_op jit(solution)/shard_map/jit(_roll_static)/slice | solution.py:530
  92.8 2.7 %fusion.3 = bf16[256,256]{1,0:T(8,128)(2,1)} fusion(f32[256,1]{1,0:T(8,128)S(1)} %get-tuple-element.7, f32[256,255]{1,0:T(8,128)S(1)} %get-tuple-element.9, f32[256,255]{1,0:T(8,128)S(1)} %get-tuple-element.8, f32[256,1]{1,0:T(8,128)S(1)} %get-tuple-element.6, f32[256]{0:T(256)S(1)} %fusion.11, f32[256]{0:T(256)S(1)} %convert_element_type.17, ...), kind=kLoop, calls=%fused_computation.5 | loop fusion | flops 786432 | bytes 788992 | tf_op jit(solution)/shard_map/convert_element_type | solution.py:591
  95.5 1.9 %copy.13 = bf16[256,1024]{1,0:T(8,128)(2,1)} copy(bf16[256,1024]{1,0:T(8,128)(2,1)} %get-tuple-element.14) | data formatting | bytes 1048576
  (2 shorter events, 0.0 us)

commit v4 on v3

--- a/solution.py
+++ b/solution.py
@@ -256,21 +256,27 @@
     kv_diag.wait_recv()
     total = kvbuf.shape[0]
     col_id = lax.broadcasted_iota(jnp.int32, (KEPT, total), 1).astype(F32)
+    group = 4
     seen = col_id <= limit
-    scale = 1.0 / math.sqrt(HD)
+    seen = jnp.concatenate([seen] * group, axis=0)
+    scale = math.log2(math.e) / math.sqrt(HD)
     keys = kvbuf[:, :HD]
     values = kvbuf[:, HD:]
-    for h in range(width // HD):
-        cols = slice(h * HD, (h + 1) * HD)
+    for first in range(0, width // HD, group):
+        heads = [slice(h * HD, (h + 1) * HD) for h in range(first, first + group)]
         s = lax.dot_general(
-            qown[1, :, cols], keys, (((1,), (1,)), ((), ())), preferred_element_type=F32
-        ) * scale
+            jnp.concatenate([qown[1, :, cols] for cols in heads], axis=0),
+            keys,
+            (((1,), (1,)), ((), ())),
+            preferred_element_type=F32,
+        )
         s = jnp.where(seen, s, -1e30)
         top = jnp.max(s, axis=1, keepdims=True)
-        e = jnp.exp(s - top)
+        e = jnp.exp2((s - top) * scale)
         den = jnp.sum(e, axis=1, keepdims=True)
-        mixed = jnp.dot(e.astype(BF), values, preferred_element_type=F32)
-        attb[0, :, cols] = (mixed / den).astype(BF)
+        mixed = jnp.dot(e.astype(BF), values, preferred_element_type=F32) / den
+        for n, cols in enumerate(heads):
+            attb[0, :, cols] = mixed[n * KEPT : (n + 1) * KEPT].astype(BF)
 
     att_cp = send(attb.at[0], attb.at[2], att_s.at[0], att_r.at[0], (ctx_peer(2), t))
     att_sib = send(attb.at[0], attb.at[1], att_s.at[1], att_r.at[1], (sib, t))
@@ -439,28 +445,28 @@
     stage_a(1)
     stage_b(0)
     stage_a(2)
+    stage_g(0)
+    stage_c(0)
     stage_b(1)
-    stage_g(0)
     stage_a(3)
+    stage_f(0)
+    stage_g(1)
+    stage_d(0)
+    stage_c(1)
     stage_b(2)
-    stage_g(1)
-    stage_c(0)
+    stage_f(1)
+    stage_g(2)
+    stage_d(1)
+    stage_c(2)
     stage_b(3)
-    stage_g(2)
-    stage_c(1)
-    stage_f(0)
+    stage_f(2)
     stage_g(3)
-    stage_c(2)
-    stage_f(1)
-    stage_d(0)
+    stage_e(1)
+    stage_d(2)
     stage_c(3)
-    stage_f(2)
-    stage_d(1)
     stage_f(3)
-    stage_d(2)
-    stage_e(1)
+    stage_e(2)
     stage_d(3)
-    stage_e(2)
 
     @pl.when(jnp.logical_not(is_root))
     def _():

time: 97.9 us -> 90.4 us (0.923)
  Pallas kernels: 88.7 us -> 81.2 us
    pallas_call x1, Pallas kernels: 88.7 us -> 81.2 us  [fused_shards(): pl.pallas_call(fused_kernel, out_shape=(jax.ShapeDtypeStruct((rows, width...]
where the time goes in v4:
time: 90.4 us; the launch traced here: 89.8 us
  Pallas kernels  81.2 us (90%)
  local copies, waits for them, and re-layouts  3.92 us (4%)
  other arithmetic  3.39 us (4%)
  between operations  1.29 us (1%)
    pallas_call x1, Pallas kernels, fused_shards(): pl.pallas_call(fused_kernel, out_shape=(jax.ShapeDtypeStruct((rows, width...  81.2 us
    convert_element_type x1, other arithmetic, fused_shards(): kept_cache = rotate_head(raw.astype(F32), positions).astype(BF)  2.7 us
    slice x2, local copies, waits for them, and re-layouts, rotate_head(): jnp.roll(raw, 1, axis=1)  2.05 us
    unnamed x1, local copies, waits for them, and re-layouts  1.87 us

profile of v4, /device:TPU:0, one launch (start us, length us, event | category | flops | bytes accessed | tf_op | source)
XLA Modules:
  0.0 89.8 jit_solution(18340378677246173609)
XLA Ops:
  1.3 0.7 convert_element_type.17
  2.0 81.2 %shard_map.104 = (bf16[256,1024]{1,0:T(8,128)(2,1)}, bf16[256,256]{1,0:T(8,128)(2,1)}) custom-call(bf16[256,1024]{1,0:T(8,128)(2,1)} %q_hbm.1, bf16[256,1024]{1,0:T(8,128)(2,1)} %r_hbm.1, bf16[256,2048]{1,0:T(8,128)(2,1)} %kv_hbm.1, bf16[1024,2048]{1,0:T(8,128)(2,1)} %w_hbm.1, bf16[8192,256]{1,0:T(8,128)(2,1)} %cw_hbm.1, f32[1,8192]{1,0:T(1,128)} %bitcast.4, ...), custom_call_target="tpu_custom_call" | custom-call | flops 6000000000 | bytes 8000000 | tf_op jit(solution)/shard_map/pallas_call | solution.py:549
  83.2 1.0 %fusion.12 = (f32[256,1]{1,0:T(8,128)S(1)}, f32[256,1]{1,0:T(8,128)S(1)}) fusion(bf16[256,256]{1,0:T(8,128)(2,1)} %get-tuple-element.5), kind=kLoop, calls=%fused_computation.20 | loop fusion | bytes 4096 | tf_op jit(solution)/shard_map/jit(_roll_static)/slice | solution.py:536
  84.2 1.1 %fusion.13 = (f32[256,255]{1,0:T(8,128)S(1)}, f32[256,255]{1,0:T(8,128)S(1)}) fusion(bf16[256,256]{1,0:T(8,128)(2,1)} %get-tuple-element.5), kind=kLoop, calls=%fused_computation.21 | loop fusion | bytes 1044480 | tf_op jit(solution)/shard_map/jit(_roll_static)/slice | solution.py:536
  85.3 2.7 %fusion.3 = bf16[256,256]{1,0:T(8,128)(2,1)} fusion(f32[256,1]{1,0:T(8,128)S(1)} %get-tuple-element.7, f32[256,255]{1,0:T(8,128)S(1)} %get-tuple-element.9, f32[256,255]{1,0:T(8,128)S(1)} %get-tuple-element.8, f32[256,1]{1,0:T(8,128)S(1)} %get-tuple-element.6, f32[256]{0:T(256)S(1)} %fusion.11, f32[256]{0:T(256)S(1)} %convert_element_type.17, ...), kind=kLoop, calls=%fused_computation.5 | loop fusion | flops 786432 | bytes 788992 | tf_op jit(solution)/shard_map/convert_element_type | solution.py:597
  88.0 1.9 %copy.13 = bf16[256,1024]{1,0:T(8,128)(2,1)} copy(bf16[256,1024]{1,0:T(8,128)(2,1)} %get-tuple-element.14) | data formatting | bytes 1048576
  (2 shorter events, 0.0 us)

commit v5 on v4

--- a/solution.py
+++ b/solution.py
@@ -1,6 +1,7 @@
 import math
 
 import jax
+import numpy as np
 import jax.numpy as jnp
 from jax import lax
 from jax.experimental import pallas as pl
@@ -117,10 +118,10 @@
 
 
 def fused_kernel(
-    q_hbm, r_hbm, kv_hbm, w_hbm, cw_hbm, gain_hbm, keep_hbm, count_ref,
+    q_hbm, r_hbm, kv_hbm, w_hbm, cw_hbm, gain_hbm, keep_hbm, count_ref, pos_ref, freq_ref,
     hid_out, cache_out,
     gain_ref, keep_ref, q_ref, r_ref, kvbuf, w_ref, cw_ref, qown, qrecv, rown, rrecv, resbuf, attb, ownp, ysend, yrecv,
-    zsum, zrecv, xrecv, hbuf, ymsg, ymsg_in, cmsg, crecv, cbuf, hpair,
+    zsum, zrecv, xrecv, hbuf, ymsg, ymsg_in, cmsg, crecv, cbuf, hpair, cos_ref, sin_ref,
     loc_sem, kv_s, kv_r, q_s, q_r, res_s, res_r, att_s, att_r, y_s, y_r, z_s, z_r, x_r,
     ag_s, ag_r, fw_s, ay_s, ay_r, cw_s, cw_r, c_s, c_r, row_s, row_r, fin_s, fin_r,
 ):
@@ -443,6 +444,15 @@
 
     stage_a(0)
     stage_a(1)
+    diagonal = lax.broadcasted_iota(jnp.int32, (rows, rows), 0) == lax.broadcasted_iota(
+        jnp.int32, (rows, rows), 1
+    )
+    at_row = jnp.sum(
+        jnp.where(diagonal, pos_ref[...].astype(F32), 0.0), axis=1, keepdims=True
+    )
+    angles = at_row * freq_ref[...]
+    cos_ref[...] = jnp.cos(angles)
+    sin_ref[...] = jnp.sin(angles)
     stage_b(0)
     stage_a(2)
     stage_g(0)
@@ -468,13 +478,21 @@
     stage_e(2)
     stage_d(3)
 
+    stage_e(3)
+    acc, squares = stage_e(0)
+
     @pl.when(jnp.logical_not(is_root))
     def _():
         row_copy(1).wait_recv()
 
     pair_copy = send(hpair.at[k], hpair.at[k], fin_s.at[0], fin_r.at[0], (sib, t))
-    stage_e(3)
-    acc, squares = stage_e(0)
+    for i in (1, 2, 3):
+        cs[i].wait_recv()
+        more, more_squares = unpacked(crecv, i - 1)
+        acc = acc + more
+        squares = squares + more_squares
+    cbuf[k] = (acc * lax.rsqrt(squares / D + EPS)).astype(BF)
+    last = send(cbuf.at[k], cbuf.at[k], fin_s.at[1], fin_r.at[1], (sib, t))
     place = [place_of(kk) for kk in range(2)]
     pair_copy.wait_recv()
     for j in range(Z):
@@ -482,18 +500,20 @@
             jnp.dot(place[0], hpair[0, j], preferred_element_type=F32)
             + jnp.dot(place[1], hpair[1, j], preferred_element_type=F32)
         ).astype(BF)
-    for i in (1, 2, 3):
-        cs[i].wait_recv()
-        more, more_squares = unpacked(crecv, i - 1)
-        acc = acc + more
-        squares = squares + more_squares
-    cbuf[k] = (acc * lax.rsqrt(squares / D + EPS)).astype(BF)
-    last = send(cbuf.at[k], cbuf.at[k], fin_s.at[1], fin_r.at[1], (sib, t))
     last.wait_recv()
-    cache_out[...] = (
-        jnp.dot(place[0], cbuf[0], preferred_element_type=F32)
-        + jnp.dot(place[1], cbuf[1], preferred_element_type=F32)
+    raw = jnp.dot(place[0], cbuf[0], preferred_element_type=F32) + jnp.dot(
+        place[1], cbuf[1], preferred_element_type=F32
+    )
+    source = lax.broadcasted_iota(jnp.int32, (HD, HD), 0)
+    target = lax.broadcasted_iota(jnp.int32, (HD, HD), 1)
+    swap = jnp.where(
+        source == target + 1, jnp.where(target % 2 == 0, -1.0, 0.0),
+        jnp.where(source == target - 1, jnp.where(target % 2 == 1, 1.0, 0.0), 0.0),
     ).astype(BF)
+    key = raw[:, :HD]
+    partner = jnp.dot(key.astype(BF), swap, preferred_element_type=F32)
+    cache_out[:, :HD] = (key * cos_ref[...] + partner * sin_ref[...]).astype(BF)
+    cache_out[:, HD:] = raw[:, HD:].astype(BF)
 
     for copy in pending:
         copy.wait_send()
@@ -524,35 +544,24 @@
                 out_copy(i, j).wait_send()
 
 
-def rotate_head(raw, position_ids):
-    column = jnp.arange(raw.shape[1], dtype=jnp.int32)
-    within = column - column % 2
-    is_key = column < HD
-    exponent = jnp.where(is_key, within, 0).astype(F32) / HD
-    frequency = jnp.power(jnp.float32(THETA), -exponent)
-    angles = position_ids.astype(F32)[:, None] * frequency[None, :]
-    cosine = jnp.where(is_key, jnp.cos(angles), 1.0)
-    sine = jnp.where(is_key, jnp.sin(angles), 0.0)
-    partner = jnp.where(column % 2 == 0, -jnp.roll(raw, -1, axis=1), jnp.roll(raw, 1, axis=1))
-    return raw * cosine + partner * sine
-
-
 def fused_shards(
     residual, queries, keys_values, out_weight, norm_gain, cache_weight, positions, keep_rows, kept_count
 ):
     rows, width = queries.shape
+    pair_first = np.arange(HD) // 2 * 2
+    frequency = jnp.asarray(np.power(THETA, -pair_first / HD).astype(np.float32)[None, :])
     feat = out_weight.shape[1]
     n_ctx = D // feat
     dma = pltpu.SemaphoreType.DMA
     vmem = pl.BlockSpec(memory_space=pltpu.VMEM)
     hbm = pl.BlockSpec(memory_space=pl.ANY)
-    kept_hidden, raw = pl.pallas_call(
+    return pl.pallas_call(
         fused_kernel,
         out_shape=(
             jax.ShapeDtypeStruct((rows, width), BF),
             jax.ShapeDtypeStruct((rows, 2 * HD), BF),
         ),
-        in_specs=[hbm] * 7 + [vmem],
+        in_specs=[hbm] * 7 + [vmem] * 3,
         out_specs=(vmem, vmem),
         scratch_shapes=[
             pltpu.VMEM((1, D), F32),
@@ -581,6 +590,8 @@
             pltpu.VMEM((3, KEPT, 256 + HD), BF),
             pltpu.VMEM((2, KEPT, 256), BF),
             pltpu.VMEM((2, Z, KEPT, 256), BF),
+            pltpu.VMEM((rows, HD), F32),
+            pltpu.VMEM((rows, HD), F32),
             dma((7,)), dma((3,)), dma((3,)), dma((2,)), dma((2,)), dma, dma((4,)),
             dma((3,)), dma((3,)), dma((4, 4)), dma((4, 4)), dma((4, 4)), dma((4, 4)), dma((4, 4)),
             dma((4, 4)), dma((4, 4)), dma((4, 4)), dma((4,)), dma((4,)), dma, dma, dma((3,)), dma((3,)),
@@ -593,9 +604,8 @@
     )(
         queries, residual, keys_values, out_weight, cache_weight,
         norm_gain[None, :], keep_rows[None, :], kept_count[None, :],
-    )
-    kept_cache = rotate_head(raw.astype(F32), positions).astype(BF)
-    return (kept_hidden, kept_cache)
+        positions[None, :], frequency,
+    )
 
 
 def solution(mesh):

time: 90.4 us -> 85.8 us (0.949)
  other arithmetic: 3.39 us -> 0 us
    convert_element_type x2 -> x0, other arithmetic: 3.38 us -> none  [the longest x1 2.7 us: fused_shards(): kept_cache = rotate_head(raw.astype(F32), positions).astype(BF)]
    slice x2 -> x0, local copies, waits for them, and re-layouts: 2.05 us -> none  [rotate_head(): jnp.roll(raw, 1, axis=1)]
    unnamed x1 -> x2, local copies, waits for them, and re-layouts: 1.87 us -> 3.44 us
where the time goes in v5:
time: 85.8 us; the launch traced here: 85.6 us
  Pallas kernels  80.9 us (94%)
  local copies, waits for them, and re-layouts  3.44 us (4%)
  between operations  1.29 us (2%)
    pallas_call x1, Pallas kernels, fused_shards(): pl.pallas_call(fused_kernel, out_shape=(jax.ShapeDtypeStruct((rows, width...  80.9 us
    unnamed x2, local copies, waits for them, and re-layouts  3.44 us

profile of v5, /device:TPU:0, one launch (start us, length us, event | category | flops | bytes accessed | tf_op | source)
XLA Modules:
  0.0 85.6 jit_solution(17044663535719765338)
XLA Ops:
  1.3 80.9 %shard_map.113 = (bf16[256,1024]{1,0:T(8,128)(2,1)}, bf16[256,256]{1,0:T(8,128)(2,1)}) custom-call(bf16[256,1024]{1,0:T(8,128)(2,1)} %q_hbm.1, bf16[256,1024]{1,0:T(8,128)(2,1)} %r_hbm.1, bf16[256,2048]{1,0:T(8,128)(2,1)} %kv_hbm.1, bf16[1024,2048]{1,0:T(8,128)(2,1)} %w_hbm.1, bf16[8192,256]{1,0:T(8,128)(2,1)} %cw_hbm.1, f32[1,8192]{1,0:T(1,128)} %bitcast.5, ...), custom_call_target="tpu_custom_call" | custom-call | flops 6000000000 | bytes 8000000 | tf_op jit(solution)/shard_map/pallas_call | solution.py:558
  82.2 1.9 %copy.15 = bf16[256,1024]{1,0:T(8,128)(2,1)} copy(bf16[256,1024]{1,0:T(8,128)(2,1)} %get-tuple-element.4) | data formatting | bytes 1048576
  84.0 1.6 %copy.16 = bf16[256,256]{1,0:T(8,128)(2,1)} copy(bf16[256,256]{1,0:T(8,128)(2,1)} %get-tuple-element.5) | data formatting | bytes 262144

commit v6 on v5

--- a/solution.py
+++ b/solution.py
@@ -461,23 +461,22 @@
     stage_a(3)
     stage_f(0)
     stage_g(1)
-    stage_d(0)
     stage_c(1)
     stage_b(2)
     stage_f(1)
     stage_g(2)
-    stage_d(1)
     stage_c(2)
     stage_b(3)
     stage_f(2)
+    stage_d(0)
     stage_g(3)
+    stage_d(1)
+    stage_c(3)
+    stage_d(2)
+    stage_f(3)
     stage_e(1)
-    stage_d(2)
-    stage_c(3)
-    stage_f(3)
     stage_e(2)
     stage_d(3)
-
     stage_e(3)
     acc, squares = stage_e(0)
 

time: 85.8 us -> 86.3 us (level)
  no operation moved by 1% of the time
where the time goes in v6:
time: 86.3 us; the launch traced here: 86.1 us
  Pallas kernels  81.4 us (94%)
  local copies, waits for them, and re-layouts  3.44 us (4%)
  between operations  1.29 us (1%)
    pallas_call x1, Pallas kernels, fused_shards(): pl.pallas_call(fused_kernel, out_shape=(jax.ShapeDtypeStruct((rows, width...  81.4 us
    unnamed x2, local copies, waits for them, and re-layouts  3.44 us

profile of v6, /device:TPU:0, one launch (start us, length us, event | category | flops | bytes accessed | tf_op | source)
XLA Modules:
  0.0 86.1 jit_solution(4982056909074800193)
XLA Ops:
  1.3 81.4 %shard_map.113 = (bf16[256,1024]{1,0:T(8,128)(2,1)}, bf16[256,256]{1,0:T(8,128)(2,1)}) custom-call(bf16[256,1024]{1,0:T(8,128)(2,1)} %q_hbm.1, bf16[256,1024]{1,0:T(8,128)(2,1)} %r_hbm.1, bf16[256,2048]{1,0:T(8,128)(2,1)} %kv_hbm.1, bf16[1024,2048]{1,0:T(8,128)(2,1)} %w_hbm.1, bf16[8192,256]{1,0:T(8,128)(2,1)} %cw_hbm.1, f32[1,8192]{1,0:T(1,128)} %bitcast.5, ...), custom_call_target="tpu_custom_call" | custom-call | flops 6000000000 | bytes 8000000 | tf_op jit(solution)/shard_map/pallas_call | solution.py:557
  82.7 1.9 %copy.15 = bf16[256,1024]{1,0:T(8,128)(2,1)} copy(bf16[256,1024]{1,0:T(8,128)(2,1)} %get-tuple-element.4) | data formatting | bytes 1048576
  84.5 1.6 %copy.16 = bf16[256,256]{1,0:T(8,128)(2,1)} copy(bf16[256,256]{1,0:T(8,128)(2,1)} %get-tuple-element.5) | data formatting | bytes 262144

commit v7 on v5

--- a/solution.py
+++ b/solution.py
@@ -416,16 +416,19 @@
         far = jnp.zeros((KEPT, 256), F32)
         acc = jnp.zeros((KEPT, 256), F32)
         squares = jnp.zeros((KEPT, 1), F32)
+        parts = []
         for q in range(Z):
             wide = hbuf[i, q].astype(F32)
             squares = squares + jnp.sum(wide * wide, axis=1, keepdims=True)
             gain = gain_ref[:, pl.ds(pl.multiple_of(first_feat + q * 256, 256), 256)]
             scaled = (wide * gain).astype(BF)
             cut = slice(q * 256, (q + 1) * 256)
+            parts.append((scaled, cut))
             far = far + jnp.dot(scaled, cw_ref[1, cut], preferred_element_type=F32)
-            acc = acc + jnp.dot(scaled, cw_ref[0, cut], preferred_element_type=F32)
         ymsg[i, :, :256], ymsg[i, :, 256:] = packed(far, squares)
         ays[i] = send(ymsg.at[i], ymsg_in.at[i], ay_s.at[i], ay_r.at[i], ydev)
+        for scaled, cut in parts:
+            acc = acc + jnp.dot(scaled, cw_ref[0, cut], preferred_element_type=F32)
         own_part[i] = acc, squares
 
     def stage_e(i):

time: 85.8 us -> 85.8 us (level)
  no operation moved by 1% of the time
where the time goes in v7:
time: 85.8 us; the launch traced here: 85.6 us
  Pallas kernels  80.9 us (94%)
  local copies, waits for them, and re-layouts  3.44 us (4%)
  between operations  1.29 us (2%)
    pallas_call x1, Pallas kernels, fused_shards(): pl.pallas_call(fused_kernel, out_shape=(jax.ShapeDtypeStruct((rows, width...  80.9 us
    unnamed x2, local copies, waits for them, and re-layouts  3.44 us

profile of v7, /device:TPU:0, one launch (start us, length us, event | category | flops | bytes accessed | tf_op | source)
XLA Modules:
  0.0 85.6 jit_solution(6348493997351545424)
XLA Ops:
  1.3 80.9 %shard_map.113 = (bf16[256,1024]{1,0:T(8,128)(2,1)}, bf16[256,256]{1,0:T(8,128)(2,1)}) custom-call(bf16[256,1024]{1,0:T(8,128)(2,1)} %q_hbm.1, bf16[256,1024]{1,0:T(8,128)(2,1)} %r_hbm.1, bf16[256,2048]{1,0:T(8,128)(2,1)} %kv_hbm.1, bf16[1024,2048]{1,0:T(8,128)(2,1)} %w_hbm.1, bf16[8192,256]{1,0:T(8,128)(2,1)} %cw_hbm.1, f32[1,8192]{1,0:T(1,128)} %bitcast.5, ...), custom_call_target="tpu_custom_call" | custom-call | flops 6000000000 | bytes 8000000 | tf_op jit(solution)/shard_map/pallas_call | solution.py:561
  82.2 1.9 %copy.15 = bf16[256,1024]{1,0:T(8,128)(2,1)} copy(bf16[256,1024]{1,0:T(8,128)(2,1)} %get-tuple-element.4) | data formatting | bytes 1048576
  84.1 1.6 %copy.16 = bf16[256,256]{1,0:T(8,128)(2,1)} copy(bf16[256,256]{1,0:T(8,128)(2,1)} %get-tuple-element.5) | data formatting | bytes 262144
